TPU v7x, 32 devices: a whole 2x2x4 slice. The times are simulated.
32 devices in a mesh: replica: 4 (over y, x), shard: 8 (over z, core).
Axes of the slice: x: 2, y: 2, z: 4, core: 2. Of those that a mesh axis runs over, the one named last changes fastest.
Arguments:
- hidden: bfloat16 [2, 32, 256, 768], P(None, ('replica', 'shard')), may hold values from -6 to 6
- encoded: bfloat16 [2, 32, 256, 768], P(None, ('replica', 'shard')), may hold values from -6 to 6
- out_grad: bfloat16 [2, 32, 256, 768], P(None, ('replica', 'shard')), may hold values from -6 to 6
- seg_start: int32 [2, 32, 13], P(None, ('replica', 'shard')), may hold values from 0 to 240, as said below
- seg_parent: int32 [2, 32, 13], P(None, ('replica', 'shard')), may hold values from 0 to 4, as said below
- bucket_of_distance: int32 [256], replicated, may hold values from 0 to 31, as said below
- norm_self: bfloat16 [768], P('shard'), may hold values from 0.5 to 1.5
- self_query: bfloat16 [768, 768], P('shard'), may hold values from -0.109375 to 0.109375
- self_key: bfloat16 [768, 768], P('shard'), may hold values from -0.109375 to 0.109375
- self_value: bfloat16 [768, 768], P('shard'), may hold values from -0.21875 to 0.21875
- self_out: bfloat16 [768, 768], P('shard'), may hold values from -0.875 to 0.875
- rel_bias: bfloat16 [32, 12], P('shard'), may hold values from -4 to 4
- norm_cross: bfloat16 [768], P('shard'), may hold values from 0.5 to 1.5
- cross_query: bfloat16 [768, 768], P('shard'), may hold values from -0.109375 to 0.109375
- cross_key: bfloat16 [768, 768], P('shard'), may hold values from -0.109375 to 0.109375
- cross_value: bfloat16 [768, 768], P('shard'), may hold values from -0.21875 to 0.21875
- cross_out: bfloat16 [768, 768], P('shard'), may hold values from -0.875 to 0.875
- norm_ff: bfloat16 [768], P('shard'), may hold values from 0.5 to 1.5
- ff_gate: bfloat16 [768, 2048], P('shard'), may hold values from -0.21875 to 0.21875
- ff_up: bfloat16 [768, 2048], P('shard'), may hold values from -0.21875 to 0.21875
- ff_down: bfloat16 [2048, 768], P('shard'), may hold values from -0.125 to 0.125
Outputs:
- layer_out: bfloat16 [2, 32, 256, 768], P(None, ('replica', 'shard'))
- grad_hidden: bfloat16 [2, 32, 256, 768], P(None, ('replica', 'shard'))
- grad_encoded: bfloat16 [2, 32, 256, 768], P(None, ('replica', 'shard'))
- grad_norm_self: float32 [768], P('shard')
- grad_self_query: float32 [768, 768], P('shard')
- grad_self_key: float32 [768, 768], P('shard')
- grad_self_value: float32 [768, 768], P('shard')
- grad_self_out: float32 [768, 768], P('shard')
- grad_rel_bias: float32 [32, 12], P('shard')
- grad_norm_cross: float32 [768], P('shard')
- grad_cross_query: float32 [768, 768], P('shard')
- grad_cross_key: float32 [768, 768], P('shard')
- grad_cross_value: float32 [768, 768], P('shard')
- grad_cross_out: float32 [768, 768], P('shard')
- grad_norm_ff: float32 [768], P('shard')
- grad_ff_gate: float32 [768, 2048], P('shard')
- grad_ff_up: float32 [768, 2048], P('shard')
- grad_ff_down: float32 [2048, 768], P('shard')
Inputs may be any that keep to these rules, and one draw needn't show every extreme that they name: `seg_start`: segment 0 is the trunk and starts at 0; the twelve other segments lie end to end after it in some order, each once. `seg_parent`: segments 0 to 4 have parent 0; each of segments 1 to 4 is the parent of exactly two of segments 5 to 12. `bucket_of_distance`: entry 0 is 0; from one distance to the next it rises by 1 or 2 until it reaches 31, and then stays.
All inputs are finite; a program needn't handle non-finite values.
Results may differ from a plain program's by a relative error of at most 0.03.
The roundings to bfloat16 on the way count: a program that leaves them out, or rounds other values in their place, can miss the bound.
Values may be sent and summed in bfloat16 or wider, within the bound.
A program may use at most 192 MiB of HBM per device.

v0:
```python
import jax
import jax.numpy as jnp
from jax import lax
from jax.sharding import PartitionSpec as P

D = 768
H = 12
DH = 64
NB = 32
NSEG = 13
TRUNK = 64
BRANCH = 16
LEAF = 16
TREE = 256


EPSILON = 1e-06
NEGATIVE = -1000000000.0


def bucket_bounds(bucket_of_distance):
    levels = jnp.arange(NB + 1, dtype=jnp.int32)
    below = (bucket_of_distance[:, None] < levels[None, :]).astype(jnp.int32)
    return jnp.sum(below, axis=0)


def tree_layout(start, parent, bounds):
    seg_index = jnp.arange(NSEG, dtype=jnp.int32)
    seg_len = jnp.where(seg_index == 0, TRUNK, jnp.where(seg_index <= 4, BRANCH, LEAF)).astype(
        jnp.int32
    )
    seg_depth = jnp.where(
        seg_index == 0, 0, jnp.where(seg_index <= 4, TRUNK, TRUNK + BRANCH)
    ).astype(jnp.int32)
    token_place = jnp.arange(TREE, dtype=jnp.int32)
    member = (
        (token_place[:, None] >= start[None, :])
        & (token_place[:, None] < (start + seg_len)[None, :])
    ).astype(jnp.int32)
    token_depth = jnp.sum(member * (seg_depth - start)[None, :], axis=1) + token_place
    parent_hot = (parent[:, None] == seg_index[None, :]).astype(jnp.int32)
    grand_parent = jnp.dot(parent_hot, parent_hot)
    ancestry = jnp.eye(NSEG, dtype=jnp.int32) + parent_hot + grand_parent
    seg_reach = jnp.dot(jnp.dot(member, ancestry), member.T)
    allowed = (seg_reach > 0) & (token_depth[None, :] <= token_depth[:, None])
    distance = jnp.clip(token_depth[:, None] - token_depth[None, :], 0, TREE - 1)
    lower = bounds[:NB]
    upper = bounds[1:]
    onehot = (
        (distance[:, :, None] >= lower[None, None, :])
        & (distance[:, :, None] < upper[None, None, :])
    ).astype(jnp.bfloat16)
    return (allowed, onehot)


def normed(values_in, gain):
    return (
        values_in
        * lax.rsqrt(jnp.mean(values_in * values_in, axis=-1, keepdims=True) + EPSILON)
        * gain
    )


def project(left, right):
    return jnp.dot(left, right, preferred_element_type=jnp.float32)


def outer_sum(left, right):
    return jnp.einsum("sd,se->de", left, right, preferred_element_type=jnp.float32)


def back_project(grad_rows, weight):
    return jnp.einsum("se,de->sd", grad_rows, weight, preferred_element_type=jnp.float32)


def split_heads(matrix):
    return matrix.reshape(matrix.shape[0], H, DH)


def attend_scores(queries, keys_in, score_bias, allowed):
    scores = jnp.einsum(
        "ihd,jhd->hij",
        split_heads(queries),
        split_heads(keys_in),
        preferred_element_type=jnp.float32,
    )
    if score_bias is not None:
        scores = jnp.where(allowed[None], scores + score_bias, NEGATIVE)
    return scores


def attend_forward(queries, keys_in, values_in, score_bias, allowed):
    scores = attend_scores(queries, keys_in, score_bias, allowed)
    row_max = jnp.max(scores, axis=-1, keepdims=True)
    shifted = jnp.exp(scores - row_max)
    row_sum = jnp.sum(shifted, axis=-1, keepdims=True)
    soft_weights = (shifted / row_sum).astype(jnp.bfloat16)
    context = jnp.einsum(
        "hij,jhd->ihd", soft_weights, split_heads(values_in), preferred_element_type=jnp.float32
    )
    return (context.reshape(queries.shape[0], D).astype(jnp.bfloat16), row_max + jnp.log(row_sum))


def attend_backward(queries, keys_in, values_in, score_bias, allowed, log_sum, grad_context):
    scores = attend_scores(queries, keys_in, score_bias, allowed)
    probs = jnp.exp(scores - log_sum)
    soft_weights = probs.astype(jnp.bfloat16)
    grad_heads = split_heads(grad_context)
    grad_values = jnp.einsum(
        "hij,ihd->jhd", soft_weights, grad_heads, preferred_element_type=jnp.float32
    )
    grad_probs = jnp.einsum(
        "ihd,jhd->hij", grad_heads, split_heads(values_in), preferred_element_type=jnp.float32
    )
    grad_scores = (
        probs * (grad_probs - jnp.sum(grad_probs * probs, axis=-1, keepdims=True))
    ).astype(jnp.bfloat16)
    grad_queries = jnp.einsum(
        "hij,jhd->ihd", grad_scores, split_heads(keys_in), preferred_element_type=jnp.float32
    )
    grad_keys = jnp.einsum(
        "hij,ihd->jhd", grad_scores, split_heads(queries), preferred_element_type=jnp.float32
    )
    return (
        grad_queries.reshape(queries.shape[0], D).astype(jnp.bfloat16),
        grad_keys.reshape(keys_in.shape[0], D).astype(jnp.bfloat16),
        grad_values.reshape(values_in.shape[0], D).astype(jnp.bfloat16),
        grad_scores,
    )


def tree_forward(weights, inputs_bf, encoder, start, parent, bounds):
    (
        gain_self,
        w_query,
        w_key,
        w_value,
        w_out,
        bias_table,
        gain_cross,
        c_query,
        c_key,
        c_value,
        c_out,
        gain_ff,
        w_gate,
        w_up,
        w_down,
    ) = weights
    allowed, onehot = tree_layout(start, parent, bounds)
    score_bias = jnp.einsum("ijb,bh->hij", onehot, bias_table, preferred_element_type=jnp.float32)
    inputs = inputs_bf.astype(jnp.float32)
    normed_self = normed(inputs, gain_self.astype(jnp.float32)).astype(jnp.bfloat16)
    self_queries = project(normed_self, w_query).astype(jnp.bfloat16)
    self_keys = project(normed_self, w_key).astype(jnp.bfloat16)
    self_values = project(normed_self, w_value).astype(jnp.bfloat16)
    self_context, self_lse = attend_forward(
        self_queries, self_keys, self_values, score_bias, allowed
    )
    after_self = inputs + project(self_context, w_out)
    normed_cross = normed(after_self, gain_cross.astype(jnp.float32)).astype(jnp.bfloat16)
    cross_queries = project(normed_cross, c_query).astype(jnp.bfloat16)
    cross_keys = project(encoder, c_key).astype(jnp.bfloat16)
    cross_values = project(encoder, c_value).astype(jnp.bfloat16)
    cross_context, cross_lse = attend_forward(cross_queries, cross_keys, cross_values, None, None)
    after_cross = after_self + project(cross_context, c_out)
    normed_ff = normed(after_cross, gain_ff.astype(jnp.float32)).astype(jnp.bfloat16)
    gate = project(normed_ff, w_gate)
    up_proj = project(normed_ff, w_up)
    inner = (jax.nn.gelu(gate, approximate=True) * up_proj).astype(jnp.bfloat16)
    layer_out = (after_cross + project(inner, w_down)).astype(jnp.bfloat16)
    saved = (
        after_self,
        after_cross,
        normed_self,
        self_queries,
        self_keys,
        self_values,
        self_context,
        self_lse,
        normed_cross,
        cross_queries,
        cross_keys,
        cross_values,
        cross_context,
        cross_lse,
        normed_ff,
        gate,
        up_proj,
        inner,
        allowed,
        onehot,
        score_bias,
    )
    return (layer_out, saved)


def tree_backward(weights, inputs_bf, encoder, grad_out, saved):
    (
        gain_self,
        w_query,
        w_key,
        w_value,
        w_out,
        bias_table,
        gain_cross,
        c_query,
        c_key,
        c_value,
        c_out,
        gain_ff,
        w_gate,
        w_up,
        w_down,
    ) = weights
    (
        after_self,
        after_cross,
        normed_self,
        self_queries,
        self_keys,
        self_values,
        self_context,
        self_lse,
        normed_cross,
        cross_queries,
        cross_keys,
        cross_values,
        cross_context,
        cross_lse,
        normed_ff,
        gate,
        up_proj,
        inner,
        allowed,
        onehot,
        score_bias,
    ) = saved
    inputs = inputs_bf.astype(jnp.float32)
    grad_w_down = outer_sum(inner, grad_out)
    grad_inner = back_project(grad_out, w_down)
    _, gelu_pull = jax.vjp(
        lambda gate_in, up_in: jax.nn.gelu(gate_in, approximate=True) * up_in, gate, up_proj
    )
    grad_gate, grad_up = gelu_pull(grad_inner)
    grad_gate = grad_gate.astype(jnp.bfloat16)
    grad_up = grad_up.astype(jnp.bfloat16)
    grad_w_gate = outer_sum(normed_ff, grad_gate)
    grad_w_up = outer_sum(normed_ff, grad_up)
    grad_normed_ff = back_project(grad_gate, w_gate) + back_project(grad_up, w_up)
    _, norm_pull = jax.vjp(normed, after_cross, gain_ff.astype(jnp.float32))
    grad_part, grad_gain_ff = norm_pull(grad_normed_ff)
    grad_after_cross = grad_out.astype(jnp.float32) + grad_part
    cross_branch = grad_after_cross.astype(jnp.bfloat16)
    grad_c_out = outer_sum(cross_context, cross_branch)
    grad_cross_context = back_project(cross_branch, c_out).astype(jnp.bfloat16)
    grad_cq, grad_ck, grad_cv, _ = attend_backward(
        cross_queries, cross_keys, cross_values, None, None, cross_lse, grad_cross_context
    )
    grad_c_query = outer_sum(normed_cross, grad_cq)
    grad_c_key = outer_sum(encoder, grad_ck)
    grad_c_value = outer_sum(encoder, grad_cv)
    grad_encoder = (back_project(grad_ck, c_key) + back_project(grad_cv, c_value)).astype(
        jnp.bfloat16
    )
    _, norm_pull = jax.vjp(normed, after_self, gain_cross.astype(jnp.float32))
    grad_part, grad_gain_cross = norm_pull(back_project(grad_cq, c_query))
    grad_after_self = grad_after_cross + grad_part
    self_branch = grad_after_self.astype(jnp.bfloat16)
    grad_w_out = outer_sum(self_context, self_branch)
    grad_self_context = back_project(self_branch, w_out).astype(jnp.bfloat16)
    grad_sq, grad_sk, grad_sv, grad_scores = attend_backward(
        self_queries, self_keys, self_values, score_bias, allowed, self_lse, grad_self_context
    )
    grad_bias_table = jnp.einsum(
        "hij,ijb->bh", grad_scores, onehot, preferred_element_type=jnp.float32
    )
    grad_w_query = outer_sum(normed_self, grad_sq)
    grad_w_key = outer_sum(normed_self, grad_sk)
    grad_w_value = outer_sum(normed_self, grad_sv)
    grad_normed_self = (
        back_project(grad_sq, w_query)
        + back_project(grad_sk, w_key)
        + back_project(grad_sv, w_value)
    )
    _, norm_pull = jax.vjp(normed, inputs, gain_self.astype(jnp.float32))
    grad_part, grad_gain_self = norm_pull(grad_normed_self)
    grad_inputs = (grad_after_self + grad_part).astype(jnp.bfloat16)
    grads = (
        grad_gain_self,
        grad_w_query,
        grad_w_key,
        grad_w_value,
        grad_w_out,
        grad_bias_table,
        grad_gain_cross,
        grad_c_query,
        grad_c_key,
        grad_c_value,
        grad_c_out,
        grad_gain_ff,
        grad_w_gate,
        grad_w_up,
        grad_w_down,
    )
    return (grad_inputs, grad_encoder, grads)


def body(
    hidden,
    encoded,
    out_grad,
    seg_start,
    seg_parent,
    bucket_of_distance,
    norm_self,
    self_query,
    self_key,
    self_value,
    self_out,
    rel_bias,
    norm_cross,
    cross_query,
    cross_key,
    cross_value,
    cross_out,
    norm_ff,
    ff_gate,
    ff_up,
    ff_down,
):
    bounds = bucket_bounds(bucket_of_distance)
    steps_count = hidden.shape[0]
    running_shard = None
    outputs_all = []
    inputs_grads = []
    encoder_grads = []
    for micro_step in range(steps_count):
        weights_now = (
            lax.all_gather(norm_self, "shard", axis=0, tiled=True),
            lax.all_gather(self_query, "shard", axis=0, tiled=True),
            lax.all_gather(self_key, "shard", axis=0, tiled=True),
            lax.all_gather(self_value, "shard", axis=0, tiled=True),
            lax.all_gather(self_out, "shard", axis=0, tiled=True),
            lax.all_gather(rel_bias, "shard", axis=0, tiled=True),
            lax.all_gather(norm_cross, "shard", axis=0, tiled=True),
            lax.all_gather(cross_query, "shard", axis=0, tiled=True),
            lax.all_gather(cross_key, "shard", axis=0, tiled=True),
            lax.all_gather(cross_value, "shard", axis=0, tiled=True),
            lax.all_gather(cross_out, "shard", axis=0, tiled=True),
            lax.all_gather(norm_ff, "shard", axis=0, tiled=True),
            lax.all_gather(ff_gate, "shard", axis=0, tiled=True),
            lax.all_gather(ff_up, "shard", axis=0, tiled=True),
            lax.all_gather(ff_down, "shard", axis=0, tiled=True),
        )

        def forward_tree(running, tree_item):
            layer_out, saved = tree_forward(
                weights_now, tree_item[0], tree_item[1], tree_item[2], tree_item[3], bounds
            )
            return (running, (layer_out, saved))

        _, (layer_outs, saved_all) = lax.scan(
            forward_tree,
            jnp.zeros((), jnp.int32),
            (
                hidden[micro_step],
                encoded[micro_step],
                seg_start[micro_step],
                seg_parent[micro_step],
            ),
        )
        weights_back = (
            lax.all_gather(norm_self, "shard", axis=0, tiled=True),
            lax.all_gather(self_query, "shard", axis=0, tiled=True),
            lax.all_gather(self_key, "shard", axis=0, tiled=True),
            lax.all_gather(self_value, "shard", axis=0, tiled=True),
            lax.all_gather(self_out, "shard", axis=0, tiled=True),
            lax.all_gather(rel_bias, "shard", axis=0, tiled=True),
            lax.all_gather(norm_cross, "shard", axis=0, tiled=True),
            lax.all_gather(cross_query, "shard", axis=0, tiled=True),
            lax.all_gather(cross_key, "shard", axis=0, tiled=True),
            lax.all_gather(cross_value, "shard", axis=0, tiled=True),
            lax.all_gather(cross_out, "shard", axis=0, tiled=True),
            lax.all_gather(norm_ff, "shard", axis=0, tiled=True),
            lax.all_gather(ff_gate, "shard", axis=0, tiled=True),
            lax.all_gather(ff_up, "shard", axis=0, tiled=True),
            lax.all_gather(ff_down, "shard", axis=0, tiled=True),
        )

        def backward_tree(running, tree_item):
            grad_inputs, grad_encoder, grads = tree_backward(
                weights_back, tree_item[0], tree_item[1], tree_item[2], tree_item[3]
            )
            return (jax.tree.map(jnp.add, running, grads), (grad_inputs, grad_encoder))

        zero_grads = tuple((jnp.zeros(weight.shape, jnp.float32) for weight in weights_back))
        micro_grads, (grad_inputs_all, grad_encoder_all) = lax.scan(
            backward_tree,
            zero_grads,
            (hidden[micro_step], encoded[micro_step], out_grad[micro_step], saved_all),
        )
        outputs_all.append(layer_outs)
        inputs_grads.append(grad_inputs_all)
        encoder_grads.append(grad_encoder_all)
        shard_part = (
            lax.psum_scatter(
                micro_grads[0].astype(jnp.bfloat16), "shard", scatter_dimension=0, tiled=True
            ).astype(jnp.float32),
            lax.psum_scatter(
                micro_grads[1].astype(jnp.bfloat16), "shard", scatter_dimension=0, tiled=True
            ).astype(jnp.float32),
            lax.psum_scatter(
                micro_grads[2].astype(jnp.bfloat16), "shard", scatter_dimension=0, tiled=True
            ).astype(jnp.float32),
            lax.psum_scatter(
                micro_grads[3].astype(jnp.bfloat16), "shard", scatter_dimension=0, tiled=True
            ).astype(jnp.float32),
            lax.psum_scatter(
                micro_grads[4].astype(jnp.bfloat16), "shard", scatter_dimension=0, tiled=True
            ).astype(jnp.float32),
            lax.psum_scatter(
                micro_grads[5].astype(jnp.bfloat16), "shard", scatter_dimension=0, tiled=True
            ).astype(jnp.float32),
            lax.psum_scatter(
                micro_grads[6].astype(jnp.bfloat16), "shard", scatter_dimension=0, tiled=True
            ).astype(jnp.float32),
            lax.psum_scatter(
                micro_grads[7].astype(jnp.bfloat16), "shard", scatter_dimension=0, tiled=True
            ).astype(jnp.float32),
            lax.psum_scatter(
                micro_grads[8].astype(jnp.bfloat16), "shard", scatter_dimension=0, tiled=True
            ).astype(jnp.float32),
            lax.psum_scatter(
                micro_grads[9].astype(jnp.bfloat16), "shard", scatter_dimension=0, tiled=True
            ).astype(jnp.float32),
            lax.psum_scatter(
                micro_grads[10].astype(jnp.bfloat16), "shard", scatter_dimension=0, tiled=True
            ).astype(jnp.float32),
            lax.psum_scatter(
                micro_grads[11].astype(jnp.bfloat16), "shard", scatter_dimension=0, tiled=True
            ).astype(jnp.float32),
            lax.psum_scatter(
                micro_grads[12].astype(jnp.bfloat16), "shard", scatter_dimension=0, tiled=True
            ).astype(jnp.float32),
            lax.psum_scatter(
                micro_grads[13].astype(jnp.bfloat16), "shard", scatter_dimension=0, tiled=True
            ).astype(jnp.float32),
            lax.psum_scatter(
                micro_grads[14].astype(jnp.bfloat16), "shard", scatter_dimension=0, tiled=True
            ).astype(jnp.float32),
        )
        running_shard = (
            shard_part
            if running_shard is None
            else jax.tree.map(jnp.add, running_shard, shard_part)
        )
    summed = (
        lax.psum(running_shard[0].astype(jnp.bfloat16), "replica").astype(jnp.float32),
        lax.psum(running_shard[1].astype(jnp.bfloat16), "replica").astype(jnp.float32),
        lax.psum(running_shard[2].astype(jnp.bfloat16), "replica").astype(jnp.float32),
        lax.psum(running_shard[3].astype(jnp.bfloat16), "replica").astype(jnp.float32),
        lax.psum(running_shard[4].astype(jnp.bfloat16), "replica").astype(jnp.float32),
        lax.psum(running_shard[5].astype(jnp.bfloat16), "replica").astype(jnp.float32),
        lax.psum(running_shard[6].astype(jnp.bfloat16), "replica").astype(jnp.float32),
        lax.psum(running_shard[7].astype(jnp.bfloat16), "replica").astype(jnp.float32),
        lax.psum(running_shard[8].astype(jnp.bfloat16), "replica").astype(jnp.float32),
        lax.psum(running_shard[9].astype(jnp.bfloat16), "replica").astype(jnp.float32),
        lax.psum(running_shard[10].astype(jnp.bfloat16), "replica").astype(jnp.float32),
        lax.psum(running_shard[11].astype(jnp.bfloat16), "replica").astype(jnp.float32),
        lax.psum(running_shard[12].astype(jnp.bfloat16), "replica").astype(jnp.float32),
        lax.psum(running_shard[13].astype(jnp.bfloat16), "replica").astype(jnp.float32),
        lax.psum(running_shard[14].astype(jnp.bfloat16), "replica").astype(jnp.float32),
    )
    return (
        jnp.stack(outputs_all),
        jnp.stack(inputs_grads),
        jnp.stack(encoder_grads),
        summed[0],
        summed[1],
        summed[2],
        summed[3],
        summed[4],
        summed[5],
        summed[6],
        summed[7],
        summed[8],
        summed[9],
        summed[10],
        summed[11],
        summed[12],
        summed[13],
        summed[14],
    )


def solution(mesh):
    placed = (
        P(None, ("replica", "shard"), None, None),
        P(None, ("replica", "shard"), None, None),
        P(None, ("replica", "shard"), None, None),
        P(None, ("replica", "shard"), None),
        P(None, ("replica", "shard"), None),
        P(),
        P("shard"),
        P("shard", None),
        P("shard", None),
        P("shard", None),
        P("shard", None),
        P("shard", None),
        P("shard"),
        P("shard", None),
        P("shard", None),
        P("shard", None),
        P("shard", None),
        P("shard"),
        P("shard", None),
        P("shard", None),
        P("shard", None),
    )
    return jax.shard_map(
        body,
        mesh=mesh,
        in_specs=placed,
        out_specs=(
            P(None, ("replica", "shard"), None, None),
            P(None, ("replica", "shard"), None, None),
            P(None, ("replica", "shard"), None, None),
            P("shard"),
            P("shard", None),
            P("shard", None),
            P("shard", None),
            P("shard", None),
            P("shard", None),
            P("shard"),
            P("shard", None),
            P("shard", None),
            P("shard", None),
            P("shard", None),
            P("shard"),
            P("shard", None),
            P("shard", None),
            P("shard", None),
        ),
        check_vma=False,
    )
```

profile of v0, /device:TPU:0, one launch (start us, length us, event | category | flops | bytes accessed | tf_op | source)
XLA Modules:
  0.0 1235.4 jit_solution(126350286949679061)
XLA Ops:
  16.9 18.6 %all-reduce.12 = (bf16[768]{0:T(1024)(128)(2,1)S(1)}, bf16[768]{0:T(1024)(128)(2,1)S(1)}, bf16[768]{0:T(1024)(128)(2,1)S(1)}) all-reduce(bf16[768]{0:T(1024)(128)(2,1)S(1)} %dynamic-update-slice, bf16[768]{0:T(1024)(128)(2,1)S(1)} %dynamic-update-slice.1, ...), channel_id=1, replica_groups=mesh['replica'=4,'shard'=8] {'shard'}, use_global_device_ids=true, to_apply=%add | all-reduce | flops 2304 | bytes 9216
  36.8 8.4 all-gather
  45.2 4.0 fusion.1
  49.2 4.9 copy.185
  56.5 4.0 fusion.3
  60.5 5.1 copy.196
  71.9 11.7 all-gather.13.cloned.1.call-done
  86.3 2.6 fusion.212
  90.7 16.8 %all-gather.19.cloned.1.call-done = bf16[768,768]{1,0:T(8,128)(2,1)} async-done(((bf16[96,768]{1,0:T(8,128)(2,1)}), bf16[768,768]{1,0:T(8,128)(2,1)}) %all-gather.19.cloned.1.call-update) | async-done | bytes 1179664 | tf_op jit(solution)/shard_map/all_gather | solution.py:344
  107.6 2.7 multiply_reduce_fusion.15
  111.5 20.0 %all-gather.23.cloned.1.call-done = bf16[768,768]{1,0:T(8,128)(2,1)} async-done(((bf16[96,768]{1,0:T(8,128)(2,1)}), bf16[768,768]{1,0:T(8,128)(2,1)}) %all-gather.23.cloned.1.call-update) | async-done | bytes 1179664 | tf_op jit(solution)/shard_map/all_gather | solution.py:347
  134.5 21.0 %all-gather.25.cloned.1.call-done = bf16[768,768]{1,0:T(8,128)(2,1)} async-done(((bf16[96,768]{1,0:T(8,128)(2,1)}), bf16[768,768]{1,0:T(8,128)(2,1)}) %all-gather.25.cloned.1.call-update) | async-done | bytes 1179664 | tf_op jit(solution)/shard_map/all_gather | solution.py:348
  158.3 21.3 %all-gather.21.cloned.1.call-done = bf16[768,768]{1,0:T(8,128)(2,1)} async-done(((bf16[96,768]{1,0:T(8,128)(2,1)}), bf16[768,768]{1,0:T(8,128)(2,1)}) %all-gather.21.cloned.1.call-update) | async-done | bytes 1179664 | tf_op jit(solution)/shard_map/all_gather | solution.py:349
  185.2 2.7 convolution_convert_fusion.37
  189.1 2.8 convolution_convert_fusion.39
  193.8 2.7 fusion.210
  202.5 2.6 convolution_convert_fusion.34
  225.5 17.7 %all-gather.29.cloned.1.call-done = bf16[768,2048]{1,0:T(8,128)(2,1)} async-done(((bf16[96,2048]{1,0:T(8,128)(2,1)}), bf16[768,2048]{1,0:T(8,128)(2,1)}) %all-gather.29.cloned.1.call-update) | async-done | bytes 3145744 | tf_op jit(solution)/shard_map/all_gather | solution.py:352
  243.2 4.2 fusion.214
  247.5 34.5 %all-gather.31.cloned.1.call-done = bf16[768,2048]{1,0:T(8,128)(2,1)} async-done(((bf16[96,2048]{1,0:T(8,128)(2,1)}), bf16[768,2048]{1,0:T(8,128)(2,1)}) %all-gather.31.cloned.1.call-update) | async-done | bytes 3145744 | tf_op jit(solution)/shard_map/all_gather | solution.py:353
  281.9 4.3 fusion.215
  286.2 34.6 %all-gather.33.cloned.1.call-done = bf16[2048,768]{1,0:T(8,128)(2,1)} async-done(((bf16[256,768]{1,0:T(8,128)(2,1)}), bf16[2048,768]{1,0:T(8,128)(2,1)}) %all-gather.33.cloned.1.call-update) | async-done | bytes 3145744 | tf_op jit(solution)/shard_map/all_gather | solution.py:354
  320.8 6.6 multiply_convert_fusion.5
  335.4 3.7 multiply_convert_fusion.4
  347.5 2.6 fusion.68
  356.2 2.8 convolution_convert_fusion.28
  361.0 2.6 fusion.74
  368.4 3.1 multiply_reduce_fusion.3
  378.8 3.1 multiply_reduce_fusion.1
  389.4 2.8 convolution_convert_fusion.7
  392.2 2.9 convolution_convert_fusion.6
  407.0 2.8 multiply_reduce_fusion.7
  413.6 2.8 convolution_convert_fusion.14
  417.8 2.8 convolution_convert_fusion.26
  422.5 2.6 fusion.77
  428.9 2.8 convolution_convert_fusion.31
  437.8 3.1 multiply_reduce_fusion
  460.7 3.9 convolution_convert_fusion.2
  464.7 4.0 convolution_convert_fusion.3
  468.8 3.9 convolution_convert_fusion.4
  473.7 3.9 convolution_convert_fusion.5
  477.7 4.0 convolution_convert_fusion
  481.7 4.0 convolution_convert_fusion.1
  487.4 3.1 copy.219
  490.5 3.1 copy.218
  504.9 27.0 %all-reduce.11 = (bf16[768]{0:T(1024)(128)(2,1)S(1)}, bf16[768]{0:T(1024)(128)(2,1)S(1)}, bf16[32,12]{1,0:T(8,128)(2,1)S(1)}, bf16[32,12]{1,0:T(8,128)(2,1)S(1)}...) all-reduce(bf16[768]{0:T(1024)(128)(2,1)S(1)} %get-tuple-element.58, ...), channel_id=3, replica_groups=mesh['replica'=4,'shard'=8] {'shard'}, use_global_device_ids=true, to_apply=%region_30.31.clone | all-reduce | flops 5376 | bytes 21504
  532.0 10.3 all-reduce.13
  554.2 31.6 %reduce-scatter.47.cloned.1.call-done = bf16[96,768]{1,0:T(8,128)(2,1)} async-done(((bf16[768,768]{1,0:T(8,128)(2,1)}), bf16[96,768]{1,0:T(8,128)(2,1)}) %reduce-scatter.47.cloned.1.call-update) | async-done | bytes 147472 | tf_op jit(solution)/shard_map/reduce_scatter | solution.py:428
  585.8 33.4 %reduce-scatter.49.cloned.1.call-done = bf16[96,768]{1,0:T(8,128)(2,1)} async-done(((bf16[768,768]{1,0:T(8,128)(2,1)}), bf16[96,768]{1,0:T(8,128)(2,1)}) %reduce-scatter.49.cloned.1.call-update) | async-done | bytes 147472 | tf_op jit(solution)/shard_map/reduce_scatter | solution.py:428
  620.9 31.5 %reduce-scatter.43.cloned.1.call-done = bf16[96,768]{1,0:T(8,128)(2,1)} async-done(((bf16[768,768]{1,0:T(8,128)(2,1)}), bf16[96,768]{1,0:T(8,128)(2,1)}) %reduce-scatter.43.cloned.1.call-update) | async-done | bytes 147472 | tf_op jit(solution)/shard_map/reduce_scatter | solution.py:419
  652.4 33.4 %reduce-scatter.45.cloned.1.call-done = bf16[96,768]{1,0:T(8,128)(2,1)} async-done(((bf16[768,768]{1,0:T(8,128)(2,1)}), bf16[96,768]{1,0:T(8,128)(2,1)}) %reduce-scatter.45.cloned.1.call-update) | async-done | bytes 147472 | tf_op jit(solution)/shard_map/reduce_scatter | solution.py:419
  687.4 31.6 %reduce-scatter.41.cloned.1.call-done = bf16[96,768]{1,0:T(8,128)(2,1)} async-done(((bf16[768,768]{1,0:T(8,128)(2,1)}), bf16[96,768]{1,0:T(8,128)(2,1)}) %reduce-scatter.41.cloned.1.call-update) | async-done | bytes 147472 | tf_op jit(solution)/shard_map/reduce_scatter | solution.py:416
  719.0 33.4 %reduce-scatter.39.cloned.1.call-done = bf16[96,768]{1,0:T(8,128)(2,1)} async-done(((bf16[768,768]{1,0:T(8,128)(2,1)}), bf16[96,768]{1,0:T(8,128)(2,1)}) %reduce-scatter.39.cloned.1.call-update) | async-done | bytes 147472 | tf_op jit(solution)/shard_map/reduce_scatter | solution.py:416
  754.0 31.6 %reduce-scatter.37.cloned.1.call-done = bf16[96,768]{1,0:T(8,128)(2,1)} async-done(((bf16[768,768]{1,0:T(8,128)(2,1)}), bf16[96,768]{1,0:T(8,128)(2,1)}) %reduce-scatter.37.cloned.1.call-update) | async-done | bytes 147472 | tf_op jit(solution)/shard_map/reduce_scatter | solution.py:413
  785.7 33.3 %reduce-scatter.35.cloned.1.call-done = bf16[96,768]{1,0:T(8,128)(2,1)} async-done(((bf16[768,768]{1,0:T(8,128)(2,1)}), bf16[96,768]{1,0:T(8,128)(2,1)}) %reduce-scatter.35.cloned.1.call-update) | async-done | bytes 147472 | tf_op jit(solution)/shard_map/reduce_scatter | solution.py:413
  820.7 31.6 %reduce-scatter.33.cloned.1.call-done = bf16[96,768]{1,0:T(8,128)(2,1)} async-done(((bf16[768,768]{1,0:T(8,128)(2,1)}), bf16[96,768]{1,0:T(8,128)(2,1)}) %reduce-scatter.33.cloned.1.call-update) | async-done | bytes 147472 | tf_op jit(solution)/shard_map/reduce_scatter | solution.py:410
  852.2 32.9 %reduce-scatter.31.cloned.1.call-done = bf16[96,768]{1,0:T(8,128)(2,1)} async-done(((bf16[768,768]{1,0:T(8,128)(2,1)}), bf16[96,768]{1,0:T(8,128)(2,1)}) %reduce-scatter.31.cloned.1.call-update) | async-done | bytes 147472 | tf_op jit(solution)/shard_map/reduce_scatter | solution.py:410
  888.2 37.8 %reduce-scatter.61.cloned.1.call-done = bf16[96,2048]{1,0:T(8,128)(2,1)} async-done(((bf16[768,2048]{1,0:T(8,128)(2,1)}), bf16[96,2048]{1,0:T(8,128)(2,1)}) %reduce-scatter.61.cloned.1.call-update) | async-done | bytes 393232 | tf_op jit(solution)/shard_map/reduce_scatter | solution.py:446
  926.1 41.8 %reduce-scatter.59.cloned.1.call-done = bf16[96,2048]{1,0:T(8,128)(2,1)} async-done(((bf16[768,2048]{1,0:T(8,128)(2,1)}), bf16[96,2048]{1,0:T(8,128)(2,1)}) %reduce-scatter.59.cloned.1.call-update) | async-done | bytes 393232 | tf_op jit(solution)/shard_map/reduce_scatter | solution.py:446
  969.8 39.6 %reduce-scatter.57.cloned.1.call-done = bf16[96,2048]{1,0:T(8,128)(2,1)} async-done(((bf16[768,2048]{1,0:T(8,128)(2,1)}), bf16[96,2048]{1,0:T(8,128)(2,1)}) %reduce-scatter.57.cloned.1.call-update) | async-done | bytes 393232 | tf_op jit(solution)/shard_map/reduce_scatter | solution.py:443
  1009.4 41.8 %reduce-scatter.55.cloned.1.call-done = bf16[96,2048]{1,0:T(8,128)(2,1)} async-done(((bf16[768,2048]{1,0:T(8,128)(2,1)}), bf16[96,2048]{1,0:T(8,128)(2,1)}) %reduce-scatter.55.cloned.1.call-update) | async-done | bytes 393232 | tf_op jit(solution)/shard_map/reduce_scatter | solution.py:443
  1053.1 39.8 %reduce-scatter.65.cloned.1.call-done = bf16[256,768]{1,0:T(8,128)(2,1)} async-done(((bf16[2048,768]{1,0:T(8,128)(2,1)}), bf16[256,768]{1,0:T(8,128)(2,1)}) %reduce-scatter.65.cloned.1.call-update) | async-done | bytes 393232 | tf_op jit(solution)/shard_map/reduce_scatter | solution.py:449
  1092.9 41.6 %reduce-scatter.63.cloned.1.call-done = bf16[256,768]{1,0:T(8,128)(2,1)} async-done(((bf16[2048,768]{1,0:T(8,128)(2,1)}), bf16[256,768]{1,0:T(8,128)(2,1)}) %reduce-scatter.63.cloned.1.call-update) | async-done | bytes 393232 | tf_op jit(solution)/shard_map/reduce_scatter | solution.py:449
  1147.7 69.6 %all-reduce.17.cloned.1.call-done = (bf16[96,768]{0,1:T(8,128)(2,1)}, bf16[96,768]{0,1:T(8,128)(2,1)}, bf16[96,768]{1,0:T(8,128)(2,1)}, bf16[96,768]{1,0:T(8,128...) async-done(((bf16[96,768]{0,1:T(8,128)(2,1)}, ...) | async-done | bytes 2359312 | tf_op jit(solution)/shard_map/psum | solution.py:467
  (595 shorter events, 219.0 us)
Async XLA Ops:
  7.2 7.7 copy-start.157
  7.2 7.7 copy-start.152
  7.2 9.0 copy-start.169
  7.2 9.2 copy-start.170
  7.2 9.4 copy-start.171
  7.2 28.3 %copy-start.11 = (bf16[2,1,256,768]{3,2,1,0:T(8,128)(2,1)S(1)}, bf16[2,1,256,768]{3,2,1,0:T(8,128)(2,1)}, u32[]{:S(2)}) copy-start(bf16[2,1,256,768]{3,2,1,0:T(8,128)(2,1)} %param.21) | copy-start | bytes 2359300
  7.3 29.3 %copy-start.168 = (s32[256]{0:T(256)S(1)}, s32[256]{0:T(256)}, u32[]{:S(2)}) copy-start(s32[256]{0:T(256)} %param.26) | copy-start | bytes 3076
  7.3 29.5 %copy-start.158 = (bf16[4,12]{1,0:T(4,128)(2,1)S(1)}, bf16[4,12]{1,0:T(4,128)(2,1)}, u32[]{:S(2)}) copy-start(bf16[4,12]{1,0:T(4,128)(2,1)} %param.32) | copy-start | bytes 292
  7.3 59.9 %all-gather.15.cloned.1.call-start = ((), (), s32[]{:S(2)}) async-start(), calls=%async_computation.23 | async-start | bytes 1327104 | tf_op jit(solution)/shard_map/all_gather | solution.py:341
  8.0 61.9 %all-gather.17.cloned.1.call-start = ((), (), s32[]{:S(2)}) async-start(), calls=%async_computation.24 | async-start | bytes 1327104 | tf_op jit(solution)/shard_map/all_gather | solution.py:342
  8.8 74.8 %all-gather.13.cloned.1.call-start = ((), (), s32[]{:S(2)}) async-start(), calls=%async_computation.22 | async-start | bytes 1327104 | tf_op jit(solution)/shard_map/all_gather | solution.py:343
  9.5 98.1 %all-gather.19.cloned.1.call-start = ((), (), s32[]{:S(2)}) async-start(), calls=%async_computation.25 | async-start | bytes 1327104 | tf_op jit(solution)/shard_map/all_gather | solution.py:344
  10.1 121.4 %all-gather.23.cloned.1.call-start = ((), (), s32[]{:S(2)}) async-start(), calls=%async_computation.27 | async-start | bytes 1327104 | tf_op jit(solution)/shard_map/all_gather | solution.py:347
  10.7 144.8 %all-gather.25.cloned.1.call-start = ((), (), s32[]{:S(2)}) async-start(), calls=%async_computation.28 | async-start | bytes 1327104 | tf_op jit(solution)/shard_map/all_gather | solution.py:348
  11.2 168.3 %all-gather.21.cloned.1.call-start = ((), (), s32[]{:S(2)}) async-start(), calls=%async_computation.26 | async-start | bytes 1327104 | tf_op jit(solution)/shard_map/all_gather | solution.py:349
  12.0 204.5 %all-gather.27.cloned.1.call-start = ((), (), s32[]{:S(2)}) async-start(), calls=%async_computation.29 | async-start | bytes 1327104 | tf_op jit(solution)/shard_map/all_gather | solution.py:350
  12.7 230.5 %all-gather.29.cloned.1.call-start = ((), (), s32[]{:S(2)}) async-start(), calls=%async_computation.30 | async-start | bytes 3538944 | tf_op jit(solution)/shard_map/all_gather | solution.py:352
  13.5 268.5 %all-gather.31.cloned.1.call-start = ((), (), s32[]{:S(2)}) async-start(), calls=%async_computation.31 | async-start | bytes 3538944 | tf_op jit(solution)/shard_map/all_gather | solution.py:353
  14.1 306.7 %all-gather.33.cloned.1.call-start = ((), (), s32[]{:S(2)}) async-start(), calls=%async_computation.32 | async-start | bytes 3538944 | tf_op jit(solution)/shard_map/all_gather | solution.py:354
  14.8 531.0 %reduce-scatter.71.cloned.1.call-start = ((), (), s32[]{:S(2)}) async-start(), calls=%async_computation.53 | async-start | bytes 1327104
  35.8 19.9 %copy-start.146 = (f32[256]{0:T(256)}, f32[256]{0:T(256)S(1)}, u32[]{:S(2)}) copy-start(f32[256]{0:T(256)S(1)} %get-tuple-element.587) | copy-start | bytes 3076
  36.6 12.6 %copy-start.111 = (s32[256,256]{1,0:T(8,128)}, s32[256,256]{1,0:T(8,128)S(1)}, u32[]{:S(2)}) copy-start(s32[256,256]{1,0:T(8,128)S(1)} %subtract_clamp_fusion.1) | copy-start | bytes 786436
  36.8 19.7 %copy-start.162 = (s32[32]{0:T(128)}, s32[32]{0:T(128)S(1)}, u32[]{:S(2)}) copy-start(s32[32]{0:T(128)S(1)} %get-tuple-element.695) | copy-start | bytes 388
  36.8 19.7 %copy-start.164 = (s32[32]{0:T(128)}, s32[32]{0:T(128)S(1)}, u32[]{:S(2)}) copy-start(s32[32]{0:T(128)S(1)} %get-tuple-element.696) | copy-start | bytes 388
  71.9 17.0 %copy-start.61 = (bf16[256,768]{0,1:T(8,128)(2,1)}, bf16[256,768]{0,1:T(8,128)(2,1)S(1)}, u32[]{:S(2)}) copy-start(bf16[256,768]{0,1:T(8,128)(2,1)S(1)} %copy.183) | copy-start | bytes 1179652
  90.7 40.8 %copy-start.103 = (bf16[12,64,256]{2,1,0:T(8,128)(2,1)}, bf16[12,64,256]{2,1,0:T(8,128)(2,1)S(1)}, u32[]{:S(2)}) copy-start(bf16[12,64,256]{2,1,0:T(8,128)(2,1)S(1)} %fusion.67) | copy-start | bytes 1179652
  189.1 7.4 copy-start.63
  205.2 6.5 copy-start.73
  218.7 6.7 copy-start.38
  218.8 6.6 copy-start.138
  225.5 56.4 %copy-start.28 = (bf16[256,768]{1,0:T(8,128)(2,1)}, bf16[256,768]{1,0:T(8,128)(2,1)S(1)}, u32[]{:S(2)}) copy-start(bf16[256,768]{1,0:T(8,128)(2,1)S(1)} %multiply_convert_fusion.10) | copy-start | bytes 1179652
  320.8 6.6 copy-start.37
  354.8 192.1 %reduce-scatter.73.cloned.1.call-start = ((), (), s32[]{:S(2)}) async-start(), calls=%async_computation.54 | async-start | bytes 1327104
  368.3 179.7 %reduce-scatter.67.cloned.1.call-start = ((), (), s32[]{:S(2)}) async-start(), calls=%async_computation.51 | async-start | bytes 1327104
  378.7 170.4 %reduce-scatter.69.cloned.1.call-start = ((), (), s32[]{:S(2)}) async-start(), calls=%async_computation.52 | async-start | bytes 1327104
  389.1 161.1 %reduce-scatter.51.cloned.1.call-start = ((), (), s32[]{:S(2)}) async-start(), calls=%async_computation.43 | async-start | bytes 1327104 | tf_op jit(solution)/shard_map/reduce_scatter | solution.py:437
  392.1 160.4 %reduce-scatter.53.cloned.1.call-start = ((), (), s32[]{:S(2)}) async-start(), calls=%async_computation.44 | async-start | bytes 1327104 | tf_op jit(solution)/shard_map/reduce_scatter | solution.py:437
  395.1 190.6 %reduce-scatter.47.cloned.1.call-start = ((), (), s32[]{:S(2)}) async-start(), calls=%async_computation.41 | async-start | bytes 1327104 | tf_op jit(solution)/shard_map/reduce_scatter | solution.py:428
  399.6 219.6 %reduce-scatter.49.cloned.1.call-start = ((), (), s32[]{:S(2)}) async-start(), calls=%async_computation.42 | async-start | bytes 1327104 | tf_op jit(solution)/shard_map/reduce_scatter | solution.py:428
  404.7 247.6 %reduce-scatter.43.cloned.1.call-start = ((), (), s32[]{:S(2)}) async-start(), calls=%async_computation.39 | async-start | bytes 1327104 | tf_op jit(solution)/shard_map/reduce_scatter | solution.py:419
  413.5 272.2 %reduce-scatter.45.cloned.1.call-start = ((), (), s32[]{:S(2)}) async-start(), calls=%async_computation.40 | async-start | bytes 1327104 | tf_op jit(solution)/shard_map/reduce_scatter | solution.py:419
  416.4 302.6 %reduce-scatter.41.cloned.1.call-start = ((), (), s32[]{:S(2)}) async-start(), calls=%async_computation.38 | async-start | bytes 1327104 | tf_op jit(solution)/shard_map/reduce_scatter | solution.py:416
  427.5 324.8 %reduce-scatter.39.cloned.1.call-start = ((), (), s32[]{:S(2)}) async-start(), calls=%async_computation.37 | async-start | bytes 1327104 | tf_op jit(solution)/shard_map/reduce_scatter | solution.py:416
  437.8 347.9 %reduce-scatter.37.cloned.1.call-start = ((), (), s32[]{:S(2)}) async-start(), calls=%async_computation.36 | async-start | bytes 1327104 | tf_op jit(solution)/shard_map/reduce_scatter | solution.py:413
  445.9 373.1 %reduce-scatter.35.cloned.1.call-start = ((), (), s32[]{:S(2)}) async-start(), calls=%async_computation.35 | async-start | bytes 1327104 | tf_op jit(solution)/shard_map/reduce_scatter | solution.py:413
  452.8 399.4 %reduce-scatter.33.cloned.1.call-start = ((), (), s32[]{:S(2)}) async-start(), calls=%async_computation.34 | async-start | bytes 1327104 | tf_op jit(solution)/shard_map/reduce_scatter | solution.py:410
  456.7 428.4 %reduce-scatter.31.cloned.1.call-start = ((), (), s32[]{:S(2)}) async-start(), calls=%async_computation.33 | async-start | bytes 1327104 | tf_op jit(solution)/shard_map/reduce_scatter | solution.py:410
  460.7 465.4 %reduce-scatter.61.cloned.1.call-start = ((), (), s32[]{:S(2)}) async-start(), calls=%async_computation.48 | async-start | bytes 3538944 | tf_op jit(solution)/shard_map/reduce_scatter | solution.py:446
  464.7 503.2 %reduce-scatter.59.cloned.1.call-start = ((), (), s32[]{:S(2)}) async-start(), calls=%async_computation.47 | async-start | bytes 3538944 | tf_op jit(solution)/shard_map/reduce_scatter | solution.py:446
  468.8 540.7 %reduce-scatter.57.cloned.1.call-start = ((), (), s32[]{:S(2)}) async-start(), calls=%async_computation.46 | async-start | bytes 3538944 | tf_op jit(solution)/shard_map/reduce_scatter | solution.py:443
  472.7 578.5 %reduce-scatter.55.cloned.1.call-start = ((), (), s32[]{:S(2)}) async-start(), calls=%async_computation.45 | async-start | bytes 3538944 | tf_op jit(solution)/shard_map/reduce_scatter | solution.py:443
  477.6 615.3 %reduce-scatter.65.cloned.1.call-start = ((), (), s32[]{:S(2)}) async-start(), calls=%async_computation.50 | async-start | bytes 3538944 | tf_op jit(solution)/shard_map/reduce_scatter | solution.py:449
  481.7 652.8 %reduce-scatter.63.cloned.1.call-start = ((), (), s32[]{:S(2)}) async-start(), calls=%async_computation.49 | async-start | bytes 3538944 | tf_op jit(solution)/shard_map/reduce_scatter | solution.py:449
  485.8 731.5 %all-reduce.17.cloned.1.call-start = ((), (), s32[]{:S(2)}) async-start(), calls=%async_computation.55 | async-start | bytes 4915200 | tf_op jit(solution)/shard_map/psum | solution.py:467
  503.0 41.4 %copy-start.45 = (bf16[768,768]{1,0:T(8,128)(2,1)S(1)}, bf16[768,768]{1,0:T(8,128)(2,1)}, u32[]{:S(2)}) copy-start(bf16[768,768]{1,0:T(8,128)(2,1)} %all-gather.25.cloned.1.call-done) | copy-start | bytes 3538948
  503.0 41.4 %copy-start.69 = (bf16[12,64,256]{2,1,0:T(8,128)(2,1)S(1)}, bf16[12,64,256]{2,1,0:T(8,128)(2,1)}, u32[]{:S(2)}) copy-start(bf16[12,64,256]{2,1,0:T(8,128)(2,1)} %copy-done.68) | copy-start | bytes 1179652
  1053.1 83.4 %copy-start.48 = (bf16[768,768]{1,0:T(8,128)(2,1)S(1)}, bf16[768,768]{1,0:T(8,128)(2,1)}, u32[]{:S(2)}) copy-start(bf16[768,768]{1,0:T(8,128)(2,1)} %all-gather.21.cloned.1.call-done) | copy-start | bytes 3538948
  1217.3 5.7 copy-start.126
  1217.3 6.4 copy-start.125
  1219.3 5.2 copy-start.124
  1219.3 5.9 copy-start.123
  1219.3 6.6 copy-start.122
  1221.3 5.4 copy-start.116
  1221.3 6.2 copy-start.115
  (142 other events, 272.5 us)
Sparse Core Ops, SparseCore 0:
  9.8 25.8 all-gather.14
  37.2 22.0 all-gather.16
  61.0 22.5 all-gather.12
  85.1 22.4 all-gather.18
  109.0 22.4 all-gather.22
  133.0 22.4 all-gather.24
  157.1 22.4 all-gather.20
  181.2 22.6 all-gather.26
  205.5 37.6 all-gather.28
  244.7 37.1 all-gather.30
  283.6 37.1 all-gather.32
  355.0 31.7 reduce-scatter.70
  389.0 30.8 reduce-scatter.72
  422.1 31.1 reduce-scatter.66
  455.4 30.9 reduce-scatter.68
  488.6 30.9 reduce-scatter.50
  521.7 30.7 reduce-scatter.52
  554.7 31.0 reduce-scatter.46
  588.0 31.1 reduce-scatter.48
  621.3 30.9 reduce-scatter.42
  654.7 31.0 reduce-scatter.44
  688.0 30.9 reduce-scatter.40
  721.3 31.0 reduce-scatter.38
  754.5 31.1 reduce-scatter.36
  787.9 30.9 reduce-scatter.34
  821.1 31.0 reduce-scatter.32
  854.4 30.6 reduce-scatter.30
  887.4 38.6 reduce-scatter.60
  928.4 39.4 reduce-scatter.58
  970.0 39.4 reduce-scatter.56
  1011.7 39.4 reduce-scatter.54
  1053.5 39.4 reduce-scatter.64
  1095.1 39.4 reduce-scatter.62
  1140.1 77.1 all-reduce.16
where the time goes:
time: 1240 us
  waiting for transfers between devices  823 us (66%)
  matrix products  191 us (15%)
  local copies, waits for them, and re-layouts  89 us (7%)
  blocking collectives  64.3 us (5%)
  other arithmetic  47.1 us (4%)
  between operations  18.7 us (2%)
    reduce_scatter x2, waiting for transfers between devices, body(): lax.psum_scatter(micro_grads[12].astype(jnp.bfloat16), 'shard', scatter_d...  81.4 us
    reduce_scatter x2, waiting for transfers between devices, body(): lax.psum_scatter(micro_grads[14].astype(jnp.bfloat16), 'shard', scatter_d...  81.4 us
    reduce_scatter x2, waiting for transfers between devices, body(): lax.psum_scatter(micro_grads[13].astype(jnp.bfloat16), 'shard', scatter_d...  79.6 us
    psum x1, waiting for transfers between devices, body(): lax.psum(running_shard[8].astype(jnp.bfloat16), 'replica')  69.6 us
    reduce_scatter x2, waiting for transfers between devices, body(): lax.psum_scatter(micro_grads[7].astype(jnp.bfloat16), 'shard', scatter_di...  65 us
    reduce_scatter x2, waiting for transfers between devices, body(): lax.psum_scatter(micro_grads[2].astype(jnp.bfloat16), 'shard', scatter_di...  65 us
    reduce_scatter x2, waiting for transfers between devices, body(): lax.psum_scatter(micro_grads[3].astype(jnp.bfloat16), 'shard', scatter_di...  64.9 us
    reduce_scatter x2, waiting for transfers between devices, body(): lax.psum_scatter(micro_grads[4].astype(jnp.bfloat16), 'shard', scatter_di...  64.9 us
  transfers between devices with their start and end apart: 34, of which 26 were waited for; matrix products, arithmetic and copies ran while one was open for 20% of the time, Pallas kernels for 0%

commit v1 on v0

--- a/solution.py
+++ b/solution.py
@@ -1,6 +1,9 @@
+import functools
 import jax
 import jax.numpy as jnp
 from jax import lax
+from jax.experimental import pallas as pl
+from jax.experimental.pallas import tpu as pltpu
 from jax.sharding import PartitionSpec as P
 
 D = 768
@@ -306,192 +309,381 @@
     return (grad_inputs, grad_encoder, grads)
 
 
+MESH = pl.DeviceIdType.MESH
+SQ, FFN = 768, 2048
+TEAM_R, TEAM_S = 4, 8
+NZ = TEAM_S // 2
+
+class Team:
+    def __init__(self, shard_count):
+        self.fold = shard_count // TEAM_S
+        r = lax.axis_index("replica")
+        s = lax.axis_index("shard")
+        self.base_r = (r // TEAM_R) * TEAM_R
+        self.q = r % TEAM_R
+        self.off_s = s % self.fold
+        self.s = s // self.fold
+        self.z = self.s // 2
+        self.c = self.s % 2
+    def dev(self, q, s):
+        return (self.base_r + q, s * self.fold + self.off_s)
+    def flip(self, q, bit):
+        if bit == 1:
+            return q + 1 - 2 * (q % 2)
+        return q + 2 - 4 * (q // 2)
+    @property
+    def qx(self): return self.flip(self.q, 1)
+    @property
+    def qy(self): return self.flip(self.q, 2)
+    @property
+    def qd(self): return 3 - self.q
+
+def rcopy(src, dst, ss, rs, dev):
+    return pltpu.make_async_remote_copy(src_ref=src, dst_ref=dst, send_sem=ss, recv_sem=rs, device_id=dev, device_id_type=MESH)
+
+def enter(devs):
+    b = pltpu.get_barrier_semaphore()
+    for d in devs:
+        pl.semaphore_signal(b, inc=1, device_id=d, device_id_type=MESH)
+    pl.semaphore_wait(b, len(devs))
+
+
+PH = 4
+def piece(bufs, p, q, z, c, half=None):
+    sq, gu, dn = bufs
+    if p < 2:
+        ref = sq.at[p * 4 + q, z, c]; n = SQ
+    elif p == 2:
+        ref = gu.at[q // 2, z, c, q % 2]; n = FFN
+    else:
+        ref = dn.at[z, c, q]; n = SQ
+    if half is not None:
+        ref = ref.at[:, pl.ds(half * (n // 2), n // 2)]
+    return ref
+def own_all(bufs, p, z, c):
+    sq, gu, dn = bufs
+    if p < 2: return sq.at[pl.ds(p * 4, 4), z, c]
+    if p == 2: return gu.at[:, z, c]
+    return dn.at[z, c]
+def sib_all(bufs, p, c):
+    sq, gu, dn = bufs
+    if p < 2: return sq.at[pl.ds(p * 4, 4), :, c]
+    if p == 2: return gu.at[:, :, c]
+    return dn.at[:, c]
+
+def gather_kernel(sharded, *refs):
+    shards = refs[:11]
+    sq, gu, dn = bufs = refs[11:14]
+    (lsem, zs, zr, xs, xr, ys, yr, dxs, dxr, dys, dyr, cs, cr) = refs[14:]
+    t = Team(sharded)
+    q, z, c = t.q, t.z, t.c
+    sib = t.dev(q, z * 2 + 1 - c)
+    xn, yn = t.dev(t.qx, t.s), t.dev(t.qy, t.s)
+    def zdev(k): return t.dev(q, ((z + k) % NZ) * 2 + c)
+    def zsrc(k): return (z + NZ - k) % NZ
+    loc = []
+    for i in range(8):
+        loc.append(pltpu.make_async_copy(shards[i], sq.at[i, z, c], lsem.at[i]))
+    for i in range(2):
+        for h in range(2):
+            loc.append(pltpu.make_async_copy(shards[8 + i].at[pl.ds(h*48,48)], gu.at[i, z, c, h], lsem.at[8 + 2*i+h]))
+    for h in range(4):
+        loc.append(pltpu.make_async_copy(shards[10].at[pl.ds(h*64,64)], dn.at[z, c, h], lsem.at[12+h]))
+    for l in loc: l.start()
+    enter([sib, xn, yn] + [zdev(k) for k in range(1, NZ)])
+    for l in loc: l.wait()
+    sends = []
+    def go(cp):
+        cp.start(); sends.append(cp)
+    def s1(p):
+        for k in range(1, NZ):
+            go(rcopy(piece(bufs, p, q, z, c), piece(bufs, p, q, z, c), zs.at[p, k], zr.at[p, k], zdev(k)))
+    def s0(p):
+        a = own_all(bufs, p, z, c)
+        go(rcopy(a, a, cs.at[p, 0], cr.at[p], sib))
+    def wrecv(ref, sem):
+        rcopy(ref, ref, sem, sem, sib).wait_recv()
+    def zstep(p, k):
+        ref = piece(bufs, p, q, zsrc(k), c)
+        wrecv(ref, zr.at[p, k])
+        go(rcopy(ref, ref, xs.at[p, k], xr.at[p, k], xn))
+        go(rcopy(ref, ref, ys.at[p, k], yr.at[p, k], yn))
+        go(rcopy(ref, ref, cs.at[p, 5 * k - 4], cr.at[p], sib))
+    def xystep(p, k):
+        ref = piece(bufs, p, t.qx, zsrc(k), c)
+        wrecv(ref, xr.at[p, k])
+        h = piece(bufs, p, t.qx, zsrc(k), c, 0)
+        go(rcopy(h, h, dys.at[p, k], dyr.at[p, k], yn))
+        go(rcopy(ref, ref, cs.at[p, 5 * k - 3], cr.at[p], sib))
+        ref = piece(bufs, p, t.qy, zsrc(k), c)
+        wrecv(ref, yr.at[p, k])
+        h = piece(bufs, p, t.qy, zsrc(k), c, 1)
+        go(rcopy(h, h, dxs.at[p, k], dxr.at[p, k], xn))
+        go(rcopy(ref, ref, cs.at[p, 5 * k - 2], cr.at[p], sib))
+    def dstep(p, k):
+        h = piece(bufs, p, t.qd, zsrc(k), c, 0)
+        wrecv(h, dyr.at[p, k])
+        go(rcopy(h, h, cs.at[p, 5 * k - 1], cr.at[p], sib))
+        h = piece(bufs, p, t.qd, zsrc(k), c, 1)
+        wrecv(h, dxr.at[p, k])
+        go(rcopy(h, h, cs.at[p, 5 * k], cr.at[p], sib))
+    s1(0); s0(0); s1(1); s0(1)
+    steps = [(p, k) for p in range(PH) for k in range(1, NZ)]
+    n = len(steps)
+    for i in range(n + 2):
+        if i < n:
+            p, k = steps[i]
+            if k == 1 and p + 2 < PH:
+                s1(p + 2); s0(p + 2)
+            zstep(p, k)
+        if 1 <= i < n + 1: xystep(*steps[i - 1])
+        if 2 <= i < n + 2: dstep(*steps[i - 2])
+    for p in range(PH):
+        wrecv(sib_all(bufs, p, 1 - c), cr.at[p])
+    for cp in sends: cp.wait_send()
+
+
+def gather(shards, shard_count):
+    D = pltpu.SemaphoreType.DMA
+    pair = [D((PH, NZ)), D((PH, NZ))]
+    return pl.pallas_call(
+        functools.partial(gather_kernel, shard_count),
+        out_shape=[jax.ShapeDtypeStruct(s, jnp.bfloat16) for s in (sq_shape(), gu_shape(), dn_shape())],
+        in_specs=[pl.BlockSpec(memory_space=pltpu.HBM)] * 11,
+        out_specs=[pl.BlockSpec(memory_space=pltpu.VMEM)] * 3,
+        scratch_shapes=[D((16,))] + pair * 5 + [D((PH, 16)), D((PH,))],
+        compiler_params=pltpu.CompilerParams(collective_id=0, has_side_effects=True, vmem_limit_bytes=50 * 2**20),
+        name="gather_weights",
+    )(*shards)
+
+
+BF = jnp.bfloat16
+ROWS = (96, 96, 48, 64)
+COLS = (SQ, SQ, FFN, SQ)
+def gview(bufs, p, q, z, c):
+    sq, gu, dn = bufs
+    if p < 2: return sq.at[p * 4 + q, z, c]
+    if p == 2: return gu.at[q // 2, z, c, q % 2]
+    return dn.at[z, c, q]
+
+class Reducer:
+    NSTAGE = 7
+    def __init__(self, t, g, rc, r1, r2, rz, fin, sems, chunks):
+        self.t, self.g = t, g
+        self.rc, self.r1, self.r2, self.rz, self.fin = rc, r1, r2, rz, fin
+        (self.s_c, self.r_c, self.s_1, self.r_1, self.s_2, self.r_2, self.s_z, self.r_z, self.s_f, self.r_f) = sems
+        self.chunks = chunks
+        self.sends = []
+        q, z, c = t.q, t.z, t.c
+        self.sib = t.dev(q, z * 2 + 1 - c)
+        self.nb = (t.dev(t.qx, t.s), t.dev(t.qy, t.s))
+        self.qn = (t.qx, t.qy)
+    def zdev(self, k):
+        t = self.t
+        return t.dev(t.q, ((t.z + k) % NZ) * 2 + t.c)
+    def go(self, src, dst, ss, rs, dev):
+        cp = rcopy(src, dst, ss, rs, dev)
+        cp.start()
+        self.sends.append(cp)
+    def wr(self, ref, sem):
+        rcopy(ref, ref, sem, sem, self.sib).wait_recv()
+    def rows(self, ch):
+        p, r0, n = ch
+        return pl.ds(r0, n)
+    def cols(self, ch, h):
+        w = COLS[ch[0]] // 2
+        return pl.ds(h * w, w)
+    def gp(self, ch, q, z, c, h=None):
+        ref = gview(self.g, ch[0], q, z, c).at[self.rows(ch)]
+        return ref if h is None else ref.at[:, self.cols(ch, h)]
+    def gall(self, ch, c):
+        p = ch[0]
+        sq, gu, dn = self.g
+        if p < 2: return sq.at[pl.ds(p * 4, 4), :, c, self.rows(ch)]
+        if p == 2: return gu.at[:, :, c, :, self.rows(ch)]
+        return dn.at[:, c, :, self.rows(ch)]
+    def gq(self, ch, q, c, h):
+        p = ch[0]
+        sq, gu, dn = self.g
+        if p < 2: return sq.at[p * 4 + q, :, c, self.rows(ch), self.cols(ch, h)]
+        if p == 2: return gu.at[q // 2, :, c, q % 2, self.rows(ch), self.cols(ch, h)]
+        return dn.at[:, c, q, self.rows(ch), self.cols(ch, h)]
+    def rcp(self, ch, q, z):
+        p = ch[0]
+        b = self.rc[p]
+        if p < 2: return b.at[q, z, self.rows(ch)]
+        if p == 2: return b.at[q // 2, z, q % 2, self.rows(ch)]
+        return b.at[z, q, self.rows(ch)]
+    def rcall(self, ch):
+        p = ch[0]
+        b = self.rc[p]
+        if p < 2: return b.at[:, :, self.rows(ch)]
+        if p == 2: return b.at[:, :, :, self.rows(ch)]
+        return b.at[:, :, self.rows(ch)]
+    def stage(self, st, i):
+        t, ch = self.t, self.chunks[i]
+        q, z, c = t.q, t.z, t.c
+        p = ch[0]
+        if st == 0:
+            self.go(self.gall(ch, 1 - c), self.rcall(ch), self.s_c.at[i], self.r_c.at[i], self.sib)
+        elif st == 1:
+            self.wr(self.rcall(ch), self.r_c.at[i])
+            @pl.loop(0, 4 * NZ)
+            def _(j):
+                a, b = self.gp(ch, j // NZ, j % NZ, c), self.rcp(ch, j // NZ, j % NZ)
+                a[...] = a[...] + b[...]
+            for h in range(2):
+                for m, qq in enumerate((self.qn[h], t.qd)):
+                    slot = (qq // 2) if h == 0 else (qq % 2)
+                    self.go(self.gq(ch, qq, c, h), self.r1[p].at[h, slot, :, self.rows(ch)],
+                            self.s_1.at[i, h, m], self.r_1.at[i, h, m], self.nb[h])
+        elif st == 2:
+            for h in range(2):
+                for m, qq in ((1, self.qn[1 - h]), (0, q)):
+                    slot = (qq // 2) if h == 0 else (qq % 2)
+                    land = self.r1[p].at[h, slot, :, self.rows(ch)]
+                    self.wr(land, self.r_1.at[i, h, m])
+                    @pl.loop(0, NZ)
+                    def _(j):
+                        a = self.gp(ch, qq, j, c, h)
+                        a[...] = a[...] + self.r1[p][h, slot, j, self.rows(ch), :]
+                    if m == 1:
+                        self.go(self.gq(ch, qq, c, h), self.r2[p].at[h, :, self.rows(ch)],
+                                self.s_2.at[i, h], self.r_2.at[i, h], self.nb[1 - h])
+        elif st == 3:
+            for h in range(2):
+                self.wr(self.r2[p].at[h, :, self.rows(ch)], self.r_2.at[i, h])
+                @pl.loop(0, NZ)
+                def _(j):
+                    a = self.gp(ch, q, j, c, h)
+                    a[...] = a[...] + self.r2[p][h, j, self.rows(ch), :]
+            for k in range(1, NZ):
+                self.go(self.gp(ch, q, (z + k) % NZ, c), self.rz[p].at[k, self.rows(ch)],
+                        self.s_z.at[i, k], self.r_z.at[i, k], self.zdev(k))
+        elif st == 4:
+            for k in range(1, NZ):
+                self.wr(self.rz[p].at[k, self.rows(ch)], self.r_z.at[i, k])
+            v = self.gp(ch, q, z, c)[...].astype(jnp.float32)
+            for k in range(1, NZ):
+                v = v + self.rz[p][k, self.rows(ch), :].astype(jnp.float32)
+            f = self.fin[p].at[q, self.rows(ch)]
+            f[...] = v.astype(BF)
+            for h in range(2):
+                self.go(f, f, self.s_f.at[i, h], self.r_f.at[i, h], self.nb[h])
+        elif st == 5:
+            for h in range(2):
+                f = self.fin[p].at[self.qn[h], self.rows(ch)]
+                self.wr(f, self.r_f.at[i, h])
+                f = f.at[:, self.cols(ch, h)]
+                self.go(f, f, self.s_f.at[i, 2 + h], self.r_f.at[i, 2 + h], self.nb[1 - h])
+        elif st == 6:
+            for h in range(2):
+                f = self.fin[p].at[t.qd, self.rows(ch)].at[:, self.cols(ch, h)]
+                self.wr(f, self.r_f.at[i, 2 + h])
+    def finish(self):
+        for cp in self.sends: cp.wait_send()
+
+def sq_shape(): return (8, NZ, 2, 96, SQ)
+def gu_shape(): return (2, NZ, 2, 2, 48, FFN)
+def dn_shape(): return (NZ, 2, 4, 64, SQ)
+def scratch(nch):
+    D = pltpu.SemaphoreType.DMA
+    V = lambda s: pltpu.VMEM(s, BF)
+    rc = [V((4, NZ, 96, SQ)), V((4, NZ, 96, SQ)), V((2, NZ, 2, 48, FFN)), V((NZ, 4, 64, SQ))]
+    r1 = [V((2, 2, NZ, ROWS[p], COLS[p] // 2)) for p in range(4)]
+    r2 = [V((2, NZ, ROWS[p], COLS[p] // 2)) for p in range(4)]
+    rz = [V((NZ, ROWS[p], COLS[p])) for p in range(4)]
+    sems = [D((nch,)), D((nch,)), D((nch, 2, 2)), D((nch, 2, 2)), D((nch, 2)), D((nch, 2)), D((nch, NZ)), D((nch, NZ)), D((nch, 4)), D((nch, 4))]
+    return rc, r1, r2, rz, sems
+CHUNKS = [(3, 0, 64), (2, 0, 48), (1, 0, 96), (0, 0, 96)]
+def reduce_kernel(sharded, chunks, *refs):
+    g = refs[0:3]
+    fin = refs[3:7]
+    rest = refs[7:]
+    rc, r1, r2, rz, sems = rest[0:4], rest[4:8], rest[8:12], rest[12:16], rest[16:26]
+    t = Team(sharded)
+    R = Reducer(t, g, rc, r1, r2, rz, fin, sems, chunks)
+    enter([R.sib, R.nb[0], R.nb[1]] + [R.zdev(k) for k in range(1, NZ)])
+    n = len(chunks)
+    for i in range(n + R.NSTAGE - 1):
+        for st in range(R.NSTAGE):
+            if 0 <= i - st < n:
+                R.stage(st, i - st)
+    R.finish()
+
+def reduce(g, shard_count, chunks=CHUNKS):
+    rc, r1, r2, rz, sems = scratch(len(chunks))
+    V = pl.BlockSpec(memory_space=pltpu.VMEM)
+    return pl.pallas_call(
+        functools.partial(reduce_kernel, shard_count, chunks),
+        out_shape=[jax.ShapeDtypeStruct((4, ROWS[p], COLS[p]), BF) for p in range(4)],
+        in_specs=[V] * 3, out_specs=[V] * 4,
+        scratch_shapes=rc + r1 + r2 + rz + sems,
+        compiler_params=pltpu.CompilerParams(collective_id=1, has_side_effects=True, vmem_limit_bytes=60 * 2**20),
+        name="reduce_grads",
+    )(*g)
+
+
+def team_rows(weight, fold):
+    if fold == 1:
+        return weight
+    n = TEAM_S * fold
+    groups = [[a * fold + b for b in range(fold)] for a in range(TEAM_S)]
+    return lax.all_gather(weight, "shard", axis=0, tiled=True, axis_index_groups=groups)
+
+
+def team_sum(grad, fold, teams_r):
+    if fold > 1:
+        groups = [[a * fold + b for b in range(fold)] for a in range(TEAM_S)]
+        grad = lax.psum_scatter(grad, "shard", scatter_dimension=0, tiled=True, axis_index_groups=groups)
+    if teams_r > 1:
+        groups = [[a * TEAM_R + b for a in range(teams_r)] for b in range(TEAM_R)]
+        grad = lax.psum(grad, "replica", axis_index_groups=groups)
+    return grad
+
+
 def body(
-    hidden,
-    encoded,
-    out_grad,
-    seg_start,
-    seg_parent,
-    bucket_of_distance,
-    norm_self,
-    self_query,
-    self_key,
-    self_value,
-    self_out,
-    rel_bias,
-    norm_cross,
-    cross_query,
-    cross_key,
-    cross_value,
-    cross_out,
-    norm_ff,
-    ff_gate,
-    ff_up,
-    ff_down,
+    replicas, shards,
+    hidden, encoded, out_grad, seg_start, seg_parent, bucket_of_distance,
+    norm_self, self_query, self_key, self_value, self_out, rel_bias,
+    norm_cross, cross_query, cross_key, cross_value, cross_out,
+    norm_ff, ff_gate, ff_up, ff_down,
 ):
     bounds = bucket_bounds(bucket_of_distance)
-    steps_count = hidden.shape[0]
-    running_shard = None
-    outputs_all = []
-    inputs_grads = []
-    encoder_grads = []
-    for micro_step in range(steps_count):
-        weights_now = (
-            lax.all_gather(norm_self, "shard", axis=0, tiled=True),
-            lax.all_gather(self_query, "shard", axis=0, tiled=True),
-            lax.all_gather(self_key, "shard", axis=0, tiled=True),
-            lax.all_gather(self_value, "shard", axis=0, tiled=True),
-            lax.all_gather(self_out, "shard", axis=0, tiled=True),
-            lax.all_gather(rel_bias, "shard", axis=0, tiled=True),
-            lax.all_gather(norm_cross, "shard", axis=0, tiled=True),
-            lax.all_gather(cross_query, "shard", axis=0, tiled=True),
-            lax.all_gather(cross_key, "shard", axis=0, tiled=True),
-            lax.all_gather(cross_value, "shard", axis=0, tiled=True),
-            lax.all_gather(cross_out, "shard", axis=0, tiled=True),
-            lax.all_gather(norm_ff, "shard", axis=0, tiled=True),
-            lax.all_gather(ff_gate, "shard", axis=0, tiled=True),
-            lax.all_gather(ff_up, "shard", axis=0, tiled=True),
-            lax.all_gather(ff_down, "shard", axis=0, tiled=True),
-        )
-
-        def forward_tree(running, tree_item):
-            layer_out, saved = tree_forward(
-                weights_now, tree_item[0], tree_item[1], tree_item[2], tree_item[3], bounds
-            )
-            return (running, (layer_out, saved))
-
-        _, (layer_outs, saved_all) = lax.scan(
-            forward_tree,
-            jnp.zeros((), jnp.int32),
-            (
-                hidden[micro_step],
-                encoded[micro_step],
-                seg_start[micro_step],
-                seg_parent[micro_step],
-            ),
-        )
-        weights_back = (
-            lax.all_gather(norm_self, "shard", axis=0, tiled=True),
-            lax.all_gather(self_query, "shard", axis=0, tiled=True),
-            lax.all_gather(self_key, "shard", axis=0, tiled=True),
-            lax.all_gather(self_value, "shard", axis=0, tiled=True),
-            lax.all_gather(self_out, "shard", axis=0, tiled=True),
-            lax.all_gather(rel_bias, "shard", axis=0, tiled=True),
-            lax.all_gather(norm_cross, "shard", axis=0, tiled=True),
-            lax.all_gather(cross_query, "shard", axis=0, tiled=True),
-            lax.all_gather(cross_key, "shard", axis=0, tiled=True),
-            lax.all_gather(cross_value, "shard", axis=0, tiled=True),
-            lax.all_gather(cross_out, "shard", axis=0, tiled=True),
-            lax.all_gather(norm_ff, "shard", axis=0, tiled=True),
-            lax.all_gather(ff_gate, "shard", axis=0, tiled=True),
-            lax.all_gather(ff_up, "shard", axis=0, tiled=True),
-            lax.all_gather(ff_down, "shard", axis=0, tiled=True),
-        )
-
-        def backward_tree(running, tree_item):
-            grad_inputs, grad_encoder, grads = tree_backward(
-                weights_back, tree_item[0], tree_item[1], tree_item[2], tree_item[3]
-            )
-            return (jax.tree.map(jnp.add, running, grads), (grad_inputs, grad_encoder))
-
-        zero_grads = tuple((jnp.zeros(weight.shape, jnp.float32) for weight in weights_back))
-        micro_grads, (grad_inputs_all, grad_encoder_all) = lax.scan(
-            backward_tree,
-            zero_grads,
-            (hidden[micro_step], encoded[micro_step], out_grad[micro_step], saved_all),
-        )
-        outputs_all.append(layer_outs)
-        inputs_grads.append(grad_inputs_all)
-        encoder_grads.append(grad_encoder_all)
-        shard_part = (
-            lax.psum_scatter(
-                micro_grads[0].astype(jnp.bfloat16), "shard", scatter_dimension=0, tiled=True
-            ).astype(jnp.float32),
-            lax.psum_scatter(
-                micro_grads[1].astype(jnp.bfloat16), "shard", scatter_dimension=0, tiled=True
-            ).astype(jnp.float32),
-            lax.psum_scatter(
-                micro_grads[2].astype(jnp.bfloat16), "shard", scatter_dimension=0, tiled=True
-            ).astype(jnp.float32),
-            lax.psum_scatter(
-                micro_grads[3].astype(jnp.bfloat16), "shard", scatter_dimension=0, tiled=True
-            ).astype(jnp.float32),
-            lax.psum_scatter(
-                micro_grads[4].astype(jnp.bfloat16), "shard", scatter_dimension=0, tiled=True
-            ).astype(jnp.float32),
-            lax.psum_scatter(
-                micro_grads[5].astype(jnp.bfloat16), "shard", scatter_dimension=0, tiled=True
-            ).astype(jnp.float32),
-            lax.psum_scatter(
-                micro_grads[6].astype(jnp.bfloat16), "shard", scatter_dimension=0, tiled=True
-            ).astype(jnp.float32),
-            lax.psum_scatter(
-                micro_grads[7].astype(jnp.bfloat16), "shard", scatter_dimension=0, tiled=True
-            ).astype(jnp.float32),
-            lax.psum_scatter(
-                micro_grads[8].astype(jnp.bfloat16), "shard", scatter_dimension=0, tiled=True
-            ).astype(jnp.float32),
-            lax.psum_scatter(
-                micro_grads[9].astype(jnp.bfloat16), "shard", scatter_dimension=0, tiled=True
-            ).astype(jnp.float32),
-            lax.psum_scatter(
-                micro_grads[10].astype(jnp.bfloat16), "shard", scatter_dimension=0, tiled=True
-            ).astype(jnp.float32),
-            lax.psum_scatter(
-                micro_grads[11].astype(jnp.bfloat16), "shard", scatter_dimension=0, tiled=True
-            ).astype(jnp.float32),
-            lax.psum_scatter(
-                micro_grads[12].astype(jnp.bfloat16), "shard", scatter_dimension=0, tiled=True
-            ).astype(jnp.float32),
-            lax.psum_scatter(
-                micro_grads[13].astype(jnp.bfloat16), "shard", scatter_dimension=0, tiled=True
-            ).astype(jnp.float32),
-            lax.psum_scatter(
-                micro_grads[14].astype(jnp.bfloat16), "shard", scatter_dimension=0, tiled=True
-            ).astype(jnp.float32),
-        )
-        running_shard = (
-            shard_part
-            if running_shard is None
-            else jax.tree.map(jnp.add, running_shard, shard_part)
-        )
-    summed = (
-        lax.psum(running_shard[0].astype(jnp.bfloat16), "replica").astype(jnp.float32),
-        lax.psum(running_shard[1].astype(jnp.bfloat16), "replica").astype(jnp.float32),
-        lax.psum(running_shard[2].astype(jnp.bfloat16), "replica").astype(jnp.float32),
-        lax.psum(running_shard[3].astype(jnp.bfloat16), "replica").astype(jnp.float32),
-        lax.psum(running_shard[4].astype(jnp.bfloat16), "replica").astype(jnp.float32),
-        lax.psum(running_shard[5].astype(jnp.bfloat16), "replica").astype(jnp.float32),
-        lax.psum(running_shard[6].astype(jnp.bfloat16), "replica").astype(jnp.float32),
-        lax.psum(running_shard[7].astype(jnp.bfloat16), "replica").astype(jnp.float32),
-        lax.psum(running_shard[8].astype(jnp.bfloat16), "replica").astype(jnp.float32),
-        lax.psum(running_shard[9].astype(jnp.bfloat16), "replica").astype(jnp.float32),
-        lax.psum(running_shard[10].astype(jnp.bfloat16), "replica").astype(jnp.float32),
-        lax.psum(running_shard[11].astype(jnp.bfloat16), "replica").astype(jnp.float32),
-        lax.psum(running_shard[12].astype(jnp.bfloat16), "replica").astype(jnp.float32),
-        lax.psum(running_shard[13].astype(jnp.bfloat16), "replica").astype(jnp.float32),
-        lax.psum(running_shard[14].astype(jnp.bfloat16), "replica").astype(jnp.float32),
-    )
-    return (
-        jnp.stack(outputs_all),
-        jnp.stack(inputs_grads),
-        jnp.stack(encoder_grads),
-        summed[0],
-        summed[1],
-        summed[2],
-        summed[3],
-        summed[4],
-        summed[5],
-        summed[6],
-        summed[7],
-        summed[8],
-        summed[9],
-        summed[10],
-        summed[11],
-        summed[12],
-        summed[13],
-        summed[14],
-    )
+    fold, teams_r = shards // TEAM_S, replicas // TEAM_R
+    big = (self_query, self_key, self_value, self_out, cross_query, cross_key, cross_value, cross_out, ff_gate, ff_up, ff_down)
+    sq, gu, dn = gather([team_rows(w, fold) for w in big], shards)
+    sq, gu, dn = sq.reshape(8, SQ, SQ), gu.reshape(2, SQ, FFN), dn.reshape(FFN, SQ)
+    small = jnp.concatenate([norm_self, norm_cross, norm_ff, rel_bias.reshape(-1)])
+    small = lax.all_gather(small, "shard", axis=0)
+    rows, brows = norm_self.shape[0], rel_bias.shape[0]
+    gains = [small[:, i * rows:(i + 1) * rows].reshape(-1) for i in range(3)]
+    bias = small[:, 3 * rows:].reshape(NB, H)
+    weights = (gains[0], sq[0], sq[1], sq[2], sq[3], bias, gains[1], sq[4], sq[5], sq[6], sq[7], gains[2], gu[0], gu[1], dn)
+
+    def one_tree(running, item):
+        layer_out, saved = tree_forward(weights, item[0], item[1], item[3], item[4], bounds)
+        grad_inputs, grad_encoder, grads = tree_backward(weights, item[0], item[1], item[2], saved)
+        return (jax.tree.map(jnp.add, running, grads), (layer_out, grad_inputs, grad_encoder))
+
+    flat = lambda v: v.reshape((-1,) + v.shape[2:])
+    zeros = tuple(jnp.zeros(w.shape, jnp.float32) for w in weights)
+    grads, outs = lax.scan(one_tree, zeros, tuple(map(flat, (hidden, encoded, out_grad, seg_start, seg_parent))))
+    layer_out, grad_hidden, grad_encoded = (v.reshape(hidden.shape) for v in outs)
+    (g_ns, g_q, g_k, g_v, g_o, g_rb, g_nc, g_cq, g_ck, g_cv, g_co, g_nf, g_g, g_u, g_d) = grads
+    gsq = jnp.stack([w.astype(BF) for w in (g_q, g_k, g_v, g_o, g_cq, g_ck, g_cv, g_co)]).reshape(sq_shape())
+    ggu = jnp.stack([g_g.astype(BF), g_u.astype(BF)]).reshape(gu_shape())
+    fin = reduce((gsq, ggu, g_d.astype(BF).reshape(dn_shape())), shards)
+    f0, f1 = fin[0], fin[1]
+    f2 = fin[2].reshape(2, 96, FFN)
+    f3 = fin[3].reshape(256, SQ)
+    parts = [f0[0], f0[1], f0[2], f0[3], f1[0], f1[1], f1[2], f1[3], f2[0], f2[1], f3]
+    (o_q, o_k, o_v, o_o, o_cq, o_ck, o_cv, o_co, o_g, o_u, o_d) = [team_sum(v.astype(jnp.float32), fold, teams_r) for v in parts]
+    gsmall = lax.psum(jnp.concatenate([g_ns, g_nc, g_nf, g_rb.reshape(-1)]), ("replica", "shard"))
+    s = lax.axis_index("shard")
+    o_ns, o_nc, o_nf = (lax.dynamic_slice(gsmall, (i * D + s * rows,), (rows,)) for i in range(3))
+    o_rb = lax.dynamic_slice(gsmall[3 * D:].reshape(NB, H), (s * brows, 0), (brows, H))
+    return (layer_out, grad_hidden, grad_encoded, o_ns, o_q, o_k, o_v, o_o, o_rb, o_nc, o_cq, o_ck, o_cv, o_co, o_nf, o_g, o_u, o_d)
 
 
 def solution(mesh):
@@ -519,7 +711,7 @@
         P("shard", None),
     )
     return jax.shard_map(
-        body,
+        functools.partial(body, mesh.shape["replica"], mesh.shape["shard"]),
         mesh=mesh,
         in_specs=placed,
         out_specs=(

time: 1240 us -> 624 us (0.50)
  waiting for transfers between devices: 823 us -> 0 us
  Pallas kernels: 0 us -> 206 us
  local copies, waits for them, and re-layouts: 89 us -> 137 us
  matrix products: 191 us -> 166 us
  between operations: 18.7 us -> 2.33 us
    reduce_scatter x18 -> x0, waiting for transfers between devices: 569 us -> none  [the longest x2 81.4 us: body(): lax.psum_scatter(micro_grads[12].astype(jnp.bfloat16), 'shard', scatter_d...]
    pallas_call x0 -> x2, Pallas kernels: none -> 206 us  [the longest x1 112 us: reduce(): pl.pallas_call(functools.partial(reduce_kernel, shard_count, chunks), out...]
    all_gather x11 -> x0, waiting for transfers between devices: 178 us -> none  [the longest x1 34.6 us: body(): lax.all_gather(ff_down, 'shard', axis=0, tiled=True)]
    psum x1 -> x0, waiting for transfers between devices: 69.6 us -> none  [body(): lax.psum(running_shard[8].astype(jnp.bfloat16), 'replica')]
    while x0 -> x477, local copies, waits for them, and re-layouts: none -> 48.7 us
    psum x1, blocking collectives: 10.3 us -> 44.5 us  [body(): lax.psum(jnp.concatenate([g_ns, g_nc, g_nf, g_rb.reshape(-1)]), ('replica...]
    unnamed x2 -> x1, blocking collectives: 45.6 us -> 18.4 us
    unnamed x361 -> x81, local copies, waits for them, and re-layouts: 49.7 us -> 27.7 us
  transfers between devices with their start and end apart: 34 -> 0, of which waited for: 26 -> 0; matrix products, arithmetic and copies ran while one was open for 20% -> 0% of each run, Pallas kernels for 0% -> 0%
where the time goes in v1:
time: 624 us; the launch traced here: 618 us
  Pallas kernels  206 us (33%)
  matrix products  166 us (27%)
  local copies, waits for them, and re-layouts  137 us (22%)
  blocking collectives  62.9 us (10%)
  other arithmetic  35.7 us (6%)
  loops' own time  8.55 us (1%)
    pallas_call x1, Pallas kernels, reduce(): pl.pallas_call(functools.partial(reduce_kernel, shard_count, chunks), out...  112 us
    pallas_call x1, Pallas kernels, gather(): pl.pallas_call(functools.partial(gather_kernel, shard_count), out_shape=[...  93.7 us
    dot_general x22, matrix products, outer_sum(): jnp.einsum('sd,se->de', left, right, preferred_element_type=jnp.float32)  49 us
    while x476, local copies, waits for them, and re-layouts  48.6 us
    psum x1, blocking collectives, body(): lax.psum(jnp.concatenate([g_ns, g_nc, g_nf, g_rb.reshape(-1)]), ('replica...  44.5 us
    dot_general x22, matrix products, project(): return jnp.dot(left, right, preferred_element_type=jnp.float32)  36.8 us
    dot_general x22, matrix products, back_project(): jnp.einsum('se,de->sd', grad_rows, weight, preferred_element_type=jnp.flo...  28.2 us
    unnamed x81, local copies, waits for them, and re-layouts  27.7 us

profile of v1, /device:TPU:0, one launch (start us, length us, event | category | flops | bytes accessed | tf_op | source)
XLA Modules:
  0.0 617.7 jit_solution(15997754622871686427)
XLA Ops:
  10.9 93.7 %gather_weights.1 = (bf16[8,4,2,96,768]{4,3,2,1,0:T(8,128)(2,1)}, bf16[2,4,2,2,48,2048]{5,4,3,2,1,0:T(8,128)(2,1)}, bf16[4,2,4,64,768]{4,3,2,1,0:T(8,128)(2,1)}) custom-call(bf16[96,768]{1,0:T(8,128)(2,1)S(1)} %copy-done.3, bf16[96,768]{1,0:T(8,128)(2,1)S(1)} %copy-done.4, bf16[96,768]{1,0:T(8,128)(2,1)S(1)} %copy-done.5, bf16[96,768]{1,0:T(8,128)(2,1)S(1)} %copy-done.6, ...), custom_call_target="tpu_custom_call" | custom-call | tf_op jit(solution)/shard_map/gather_weights/pallas_call | solution.py:449
  104.7 6.9 %fusion.116 = (bf16[1,4,2,96,768]{4,3,2,1,0:T(8,128)(2,1)}, bf16[1,4,2,96,768]{4,3,2,1,0:T(8,128)(2,1)}, bf16[1,4,2,96,768]{4,3,2,1,0:T(8,128)(2,1)}, bf16[1,4,2...) fusion(bf16[8,4,2,96,768]{4,3,2,1,0:T(8,128)(2,1)} %get-tuple-e, ...), kind=kLoop, calls=%fused_computation.209 | loop fusion | bytes 18874368 | tf_op jit(solution)/shard_map/slice | solution.py:662
  113.3 18.4 %all-reduce = bf16[2688]{0:T(1024)(128)(2,1)S(1)} all-reduce(bf16[2688]{0:T(1024)(128)(2,1)S(1)} %dynamic-update-slice), channel_id=2, replica_groups=mesh['replica'=4,'shard'=8] {'shard'}, use_global_device_ids=true, to_apply=%add | all-reduce | flops 2688 | bytes 10752
  133.9 6.7 %fusion.117 = (bf16[1,4,2,2,48,2048]{5,4,3,2,1,0:T(8,128)(2,1)}, bf16[1,4,2,2,48,2048]{5,4,3,2,1,0:T(8,128)(2,1)}) fusion(bf16[2,4,2,2,48,2048]{5,4,3,2,1,0:T(8,128)(2,1)} %get-tuple-element.529), kind=kLoop, calls=%fused_computation.210 | loop fusion | bytes 12582912 | tf_op jit(solution)/shard_map/slice | solution.py:662
  142.2 282.9 %while.47 = (s32[]{:T(128)}, f32[768]{0:T(1024)}, f32[768,768]{1,0:T(8,128)}, f32[768,768]{1,0:T(8,128)}, f32[768,768]{1,0:T(8,128)}, /*index=5*/f32[768,768]{1,...) while((s32[]{:T(128)}, f32[768]{0:T(1024)}, ...), condition=%wide.region_18.19_spmd.clone, body=%wide.region_1.18_spmd.clone.sunk | while | flops 15898177536 | bytes 694531136 | solution.py:671
  147.0 4.6 fusion.412
  151.5 5.2 copy.128
  157.6 1.8 convolution_convert_fusion.24
  159.6 1.9 convolution_convert_fusion.25
  162.5 2.6 fusion.415
  166.4 2.3 convolution_convert_fusion.26
  175.9 2.6 convolution_convert_fusion.29
  186.6 2.7 fusion.421
  195.6 3.8 multiply_convert_fusion.17
  200.8 1.8 multiply_reduce_fusion.16
  205.1 1.9 copy.135
  207.9 2.9 fusion.432
  220.2 1.9 copy.136
  228.1 1.9 fusion.428
  230.0 1.8 convolution_add_fusion.11
  231.8 1.8 fusion.430
  233.7 2.2 fusion.434
  235.9 3.1 select_add_fusion.35
  241.5 3.6 select_add_fusion.37
  245.2 1.8 select_add_fusion.38
  248.1 2.4 copy-done.62
  254.7 1.9 copy-done.79
  263.4 3.1 select_add_fusion.28
  266.5 3.3 copy.137
  269.8 3.7 fusion.431
  273.6 3.7 select_add_fusion.39
  282.1 4.6 fusion.412
  286.7 5.4 copy.128
  293.0 1.8 convolution_convert_fusion.24
  295.0 1.9 convolution_convert_fusion.25
  297.9 2.6 fusion.415
  301.8 2.3 convolution_convert_fusion.26
  311.2 2.6 convolution_convert_fusion.29
  315.0 1.8 fusion.419
  321.9 2.7 fusion.421
  331.0 3.5 multiply_convert_fusion.17
  335.9 1.8 multiply_reduce_fusion.16
  340.1 1.9 copy.135
  343.0 2.9 fusion.432
  355.2 1.9 copy.136
  363.1 1.9 fusion.428
  365.0 1.8 convolution_add_fusion.11
  366.9 1.8 fusion.430
  368.7 2.2 fusion.434
  370.9 3.9 select_add_fusion.35
  377.4 6.6 %select_add_fusion.37 = f32[768,2048]{1,0:T(8,128)} fusion(f32[768,2048]{1,0:T(8,128)} %get-tuple-element.1256, bf16[256,768]{1,0:T(8,128)(2,1)S(1)} %multiply_convert_fusion.16, bf16[256,2048]{1,0:T(8,128)(2,1)S(1)} %copy-done.97, pred[]{:T(512)S(6)} %compare.3), kind=kOutput, calls=%fused_computation.5.clone.1 | convolution fusion | flops 808452096 | bytes 14024705 | tf_op jit(solution)/shard_map/while/body/eval_jaxpr/sd,se->de/dot_general | solution.py:72
  384.0 1.8 select_add_fusion.38
  387.0 2.4 copy-done.62
  393.5 1.9 copy-done.79
  402.2 3.9 select_add_fusion.28
  406.1 3.3 copy.137
  409.5 3.7 fusion.431
  413.3 6.5 %select_add_fusion.39 = f32[2048,768]{1,0:T(8,128)} fusion(f32[2048,768]{1,0:T(8,128)} %get-tuple-element.1258, bf16[256,2048]{1,0:T(8,128)(2,1)S(1)} %copy-done.95, pred[]{:T(512)S(6)} %compare.3, bf16[2,256,768]{2,1,0:T(8,128)(2,1)S(1)} %copy-done.83, s32[]{:T(128)} %get-tuple-element.1243), kind=kOutput, calls=%fused_computation.3.clone.1 | convolution fusion | flops 808452096 | bytes 14024709 | tf_op jit(solution)/shard_map/while/body/eval_jaxpr/sd,se->de/dot_general | solution.py:72
  425.1 3.4 convert_element_type.467
  430.2 3.2 pad_maximum_fusion.refs_1_
  433.4 1.8 convert_element_type.459
  451.9 2.0 convert_element_type.469
  453.9 112.1 %reduce_grads.1 = (bf16[4,96,768]{2,1,0:T(8,128)(2,1)}, bf16[4,96,768]{2,1,0:T(8,128)(2,1)}, bf16[4,48,2048]{2,1,0:T(8,128)(2,1)}, bf16[4,64,768]{2,1,0:T(8,128)(2,1)}) custom-call(bf16[8,4,2,96,768]{4,3,2,1,0:T(8,128)(2,1)} %constant_dynamic-update-slice_fusion.refs_0_, bf16[2,4,2,2,48,2048]{5,4,3,2,1,0:T(8,128)(2,1)} %pad_maximum_fusion.refs_1_, ...), custom_call_target="tpu_custom_call" | custom-call | tf_op jit(solution)/shard_map/reduce_grads/pallas_call | solution.py:617
  571.4 44.5 %psum.7 = f32[2688]{0:T(1024)S(1)} all-reduce(f32[2688]{0:T(1024)S(1)} %pad_maximum_fusion.1), channel_id=1, replica_groups=mesh['replica'=4,'shard'=8] {'replica','shard'}, use_global_device_ids=true, to_apply=%region_19.20 | all-reduce | flops 2688 | bytes 21504 | tf_op jit(solution)/shard_map/psum | solution.py:682
  (731 shorter events, 164.2 us)
Async XLA Ops:
  104.6 7.0 %copy-start.149 = (u32[32]{0:T(128)S(1)}, u32[32]{0:T(128)}, u32[]{:S(2)}) copy-start(u32[32]{0:T(128)} %constant.163) | copy-start | bytes 388
  104.6 8.2 %copy-start.145 = (bf16[4,12]{1,0:T(4,128)(2,1)S(1)}, bf16[4,12]{1,0:T(4,128)(2,1)}, u32[]{:S(2)}) copy-start(bf16[4,12]{1,0:T(4,128)(2,1)} %param.34) | copy-start | bytes 292
  104.6 8.3 %copy-start.140 = (bf16[96]{0:T(256)(128)(2,1)S(1)}, bf16[96]{0:T(256)(128)(2,1)}, u32[]{:S(2)}) copy-start(bf16[96]{0:T(256)(128)(2,1)} %param.40) | copy-start | bytes 580
  104.7 8.3 %copy-start.141 = (bf16[96]{0:T(256)(128)(2,1)S(1)}, bf16[96]{0:T(256)(128)(2,1)}, u32[]{:S(2)}) copy-start(bf16[96]{0:T(256)(128)(2,1)} %param.35) | copy-start | bytes 580
  104.7 8.3 %copy-start.142 = (bf16[96]{0:T(256)(128)(2,1)S(1)}, bf16[96]{0:T(256)(128)(2,1)}, u32[]{:S(2)}) copy-start(bf16[96]{0:T(256)(128)(2,1)} %param.29) | copy-start | bytes 580
  133.9 7.6 %copy-start.146 = (s32[256]{0:T(256)S(1)}, s32[256]{0:T(256)}, u32[]{:S(2)}) copy-start(s32[256]{0:T(256)} %param.28) | copy-start | bytes 3076
  133.9 8.3 %copy-start.26 = (bf16[2,1,256,768]{3,2,1,0:T(8,128)(2,1)S(1)}, bf16[2,1,256,768]{3,2,1,0:T(8,128)(2,1)}, u32[]{:S(2)}) copy-start(bf16[2,1,256,768]{3,2,1,0:T(8,128)(2,1)} %param.23) | copy-start | bytes 2359300
  156.9 4.6 copy-start.107
  157.6 3.9 copy-start.101
  159.6 5.6 copy-start.45
  179.7 4.5 copy-start.52
  190.0 12.7 %copy-start.24 = (f32[256,768]{1,0:T(8,128)}, f32[256,768]{1,0:T(8,128)S(1)}, u32[]{:S(2)}) copy-start(f32[256,768]{1,0:T(8,128)S(1)} %get-tuple-element.1181) | copy-start | bytes 2359300 | tf_op jit(solution)/shard_map/while
  207.0 3.8 copy-start.12
  207.0 3.9 copy-start.55
  207.0 3.9 copy-start.89
  224.5 7.3 %copy-start.50 = (bf16[12,64,256]{2,1,0:T(8,128)(2,1)}, bf16[12,64,256]{2,1,0:T(8,128)(2,1)S(1)}, u32[]{:S(2)}) copy-start(bf16[12,64,256]{2,1,0:T(8,128)(2,1)S(1)} %fusion.429) | copy-start | bytes 1179652 | tf_op jit(solution)/shard_map/while
  228.1 3.7 copy-start.85
  228.1 3.7 copy-start.103
  228.1 3.7 copy-start.109
  231.8 4.0 copy-start.58
  239.0 6.1 slice-start
  240.2 5.0 copy-start.126
  240.2 5.0 copy-start.129
  247.0 7.3 %copy-start.29 = (f32[768,2048]{1,0:T(8,128)}, f32[768,2048]{1,0:T(8,128)S(1)}, u32[]{:S(2)}) copy-start(f32[768,2048]{1,0:T(8,128)S(1)} %select_add_fusion.38) | copy-start | bytes 18874372 | tf_op jit(solution)/shard_map/while
  247.2 3.7 copy-start.91
  254.4 3.8 copy-start.60
  269.8 3.7 copy-start.83
  269.8 3.7 copy-start.95
  273.6 3.7 copy-start.138
  273.6 3.7 copy-start.28
  292.3 4.6 copy-start.107
  293.0 3.9 copy-start.101
  295.0 5.5 copy-start.45
  315.0 4.5 copy-start.52
  325.3 12.4 %copy-start.24 = (f32[256,768]{1,0:T(8,128)}, f32[256,768]{1,0:T(8,128)S(1)}, u32[]{:S(2)}) copy-start(f32[256,768]{1,0:T(8,128)S(1)} %get-tuple-element.1181) | copy-start | bytes 2359300 | tf_op jit(solution)/shard_map/while
  342.1 3.8 copy-start.12
  342.1 3.9 copy-start.55
  342.1 3.9 copy-start.89
  359.6 7.3 %copy-start.50 = (bf16[12,64,256]{2,1,0:T(8,128)(2,1)}, bf16[12,64,256]{2,1,0:T(8,128)(2,1)S(1)}, u32[]{:S(2)}) copy-start(bf16[12,64,256]{2,1,0:T(8,128)(2,1)S(1)} %fusion.429) | copy-start | bytes 1179652 | tf_op jit(solution)/shard_map/while
  363.1 3.7 copy-start.85
  363.1 3.7 copy-start.103
  363.1 3.7 copy-start.109
  366.9 4.0 copy-start.58
  370.9 3.9 copy-start.16
  370.9 3.9 copy-start.49
  370.9 3.9 copy-start.75
  370.9 3.9 copy-start.106
  370.9 3.9 copy-start.112
  374.9 9.0 %slice-start = ((s8[6291456]{0:T(1024)(128)(4,1)}), s8[4194304]{0:T(1024)(128)(4,1)S(1)}, s32[]{:S(2)}) async-start(s8[6291456]{0:T(1024)(128)(4,1)} %bitcast.481), calls=%async_computation | async-start | bytes 8388608 | tf_op jit(solution)/shard_map/while
  376.1 7.9 %copy-start.126 = (f32[768]{0:T(1024)}, f32[768]{0:T(1024)S(1)}, u32[]{:S(2)}) copy-start(f32[768]{0:T(1024)S(1)} %get-tuple-element.1297) | copy-start | bytes 9220 | tf_op jit(solution)/shard_map/while
  376.1 7.9 %copy-start.129 = (f32[768]{0:T(1024)}, f32[768]{0:T(1024)S(1)}, u32[]{:S(2)}) copy-start(f32[768]{0:T(1024)S(1)} %get-tuple-element.1292) | copy-start | bytes 9220 | tf_op jit(solution)/shard_map/while
  377.4 6.6 %slice-start.1 = ((s8[6291456]{0:T(1024)(128)(4,1)}), s8[2097152]{0:T(1024)(128)(4,1)S(1)}, s32[]{:S(2)}) async-start(s8[6291456]{0:T(1024)(128)(4,1)} %bitcast.481), calls=%async_computation.1 | async-start | bytes 4194304 | tf_op jit(solution)/shard_map/while
  377.4 6.6 %copy-start.42 = (bf16[256,2048]{1,0:T(8,128)(2,1)S(1)}, bf16[256,2048]{1,0:T(8,128)(2,1)}, u32[]{:S(2)}) copy-start(bf16[256,2048]{1,0:T(8,128)(2,1)} %copy-done.41) | copy-start | bytes 3145732 | tf_op jit(solution)/shard_map/while
  385.8 7.3 %copy-start.29 = (f32[768,2048]{1,0:T(8,128)}, f32[768,2048]{1,0:T(8,128)S(1)}, u32[]{:S(2)}) copy-start(f32[768,2048]{1,0:T(8,128)S(1)} %select_add_fusion.38) | copy-start | bytes 18874372 | tf_op jit(solution)/shard_map/while
  386.0 3.7 copy-start.91
  393.2 3.7 copy-start.60
  402.2 3.9 copy-start.123
  402.2 3.9 copy-start.18
  409.5 3.7 copy-start.83
  409.5 3.7 copy-start.95
  413.2 6.6 %copy-start.138 = (f32[32,12]{0,1:T(8,128)}, f32[32,12]{0,1:T(8,128)S(1)}, u32[]{:S(2)}) copy-start(f32[32,12]{0,1:T(8,128)S(1)} %fusion.431) | copy-start | bytes 4612 | tf_op jit(solution)/shard_map/while
  413.2 6.5 %copy-start.28 = (bf16[2,1,256,768]{3,2,1,0:T(8,128)(2,1)S(1)}, bf16[2,1,256,768]{3,2,1,0:T(8,128)(2,1)}, u32[]{:S(2)}) copy-start(bf16[2,1,256,768]{3,2,1,0:T(8,128)(2,1)} %get-tuple-element.1369) | copy-start | bytes 2359300 | tf_op jit(solution)/shard_map/while
  425.1 4.6 copy-start.30
  446.3 5.6 slice-start.2
  (209 other events, 398.2 us)
